TPU v7x, 32 devices: a whole 2x2x4 slice. The times are simulated.
32 devices in a mesh: grp: 2 (over x), date: 16 (over z, y, core).
Axes of the slice: x: 2, y: 2, z: 4, core: 2. Of those that a mesh axis runs over, the one named last changes fastest.
Arguments:
- slc: bfloat16 [96, 2, 16, 512], P('date', None, 'grp'), parts along dimension 2, may hold values from -30 to 30
- line_mask: int32 [96, 16], P('date', 'grp'), parts along dimension 1, may hold values 0 or 1
- pair_dev: int32 [400, 2], P('date'), may hold values from 0 to 15, all different within a row; in each aligned block of 25 rows (0 to 24, 25 to 49, ...) at most 5 rows name the same one
- pair_slot: int32 [400, 2], P('date'), may hold values from 0 to 5
Outputs:
- solution: float32 [96, 16, 512], P('date', 'grp'), parts along dimension 1
- residual: float32 [96, 16, 512], P('date', 'grp'), parts along dimension 1
There are 2 independent parts, one for each index of `grp`. A program takes and returns all parts, laid end to end along the dimension named above; an argument that names none is the same for every part. Nothing has to cross between parts.
Inputs may be any that keep to these rules, and one draw needn't show every extreme that they name: `pair_dev`: of the 25 rows held by one device of date, at most 5 name any one device; some device is named by exactly 5 of them; the two columns of a row differ.
All inputs are finite; a program needn't handle non-finite values. No bound on the sum of `line_mask` on one device may be relied on, other than what follows from the above.
Results may differ from a plain program's by a relative error of at most 0.0003.
Values may be sent and summed in bfloat16 or wider, within the bound.
No kernel may reach another device: no remote copies, remote signals or barrier semaphores. Data moves between devices by JAX's collectives and lax.ppermute only.
A program may use at most 128 MiB of HBM per device.

v0:
```python
import jax
import jax.numpy as jnp
from jax import lax
from jax.sharding import PartitionSpec as P

ITERS = 2


DAMPING = 0.5
EPSILON = 1e-06


def multilook(field):
    lead = [(0, 0)] * (field.ndim - 2)
    padded = jnp.pad(field, lead + [(1, 1), (4, 4)])
    row_sums = padded[..., 0:-2, :] + padded[..., 1:-1, :] + padded[..., 2:, :]
    width = field.shape[-1]
    total = row_sums[..., :, 0:width]
    for offset in range(1, 9):
        total = total + row_sums[..., :, offset : offset + width]
    return total


def coherence(first, second):
    ref_real = first[:, 0].astype(jnp.float32)
    ref_imag = first[:, 1].astype(jnp.float32)
    sec_real = second[:, 0].astype(jnp.float32)
    sec_imag = second[:, 1].astype(jnp.float32)
    inter_real = ref_real * sec_real + ref_imag * sec_imag
    inter_imag = ref_imag * sec_real - ref_real * sec_imag
    power_ref = ref_real * ref_real + ref_imag * ref_imag
    power_sec = sec_real * sec_real + sec_imag * sec_imag
    scale = jnp.sqrt(jnp.maximum(multilook(power_ref) * multilook(power_sec), 1.0))
    coh_real = multilook(inter_real) / scale
    coh_imag = multilook(inter_imag) / scale
    return (coh_real * coh_real + coh_imag * coh_imag, coh_imag)


def squares(field):
    return lax.psum(jnp.sum(field * field, axis=0), "date")


def curvature(direction, image):
    return lax.psum(jnp.sum(direction * image, axis=0), "date")


def shards(slc, line_mask, pair_dev, pair_slot):
    date_count = lax.axis_size("date")
    local_dates = slc.shape[0]
    pair_count = pair_dev.shape[0]
    slot_cap = (2 * pair_count + date_count - 1) // date_count + 1
    masked = slc * line_mask[:, None, :, None].astype(jnp.bfloat16)
    end_dev = pair_dev.reshape(-1)
    end_slot = pair_slot.reshape(-1)
    end_count = end_dev.shape[0]
    end_dates = end_dev * local_dates + end_slot
    order = jnp.arange(end_count, dtype=jnp.int32)
    earlier = (end_dev[None, :] == end_dev[:, None]) & (order[None, :] < order[:, None])
    slot_rank = jnp.sum(earlier.astype(jnp.int32), axis=1)
    slot_place = end_dev * slot_cap + slot_rank
    request = jnp.full((date_count * slot_cap,), -1, jnp.int32).at[slot_place].set(end_slot)
    wanted = lax.all_to_all(request, "date", split_axis=0, concat_axis=0, tiled=True)
    is_valid = wanted >= 0
    local_slot = jnp.clip(wanted, 0, local_dates - 1)
    slot_hits = (
        (local_slot[:, None] == jnp.arange(local_dates, dtype=jnp.int32)[None, :])
        & is_valid[:, None]
    ).astype(jnp.float32)
    empty_tiles = jnp.zeros((end_count,) + masked.shape[1:], jnp.bfloat16)
    shard_piece = lax.all_gather(masked, "date", axis=0, tiled=True)
    row_count = shard_piece.shape[0]
    inside = (end_dates >= 0) & (end_dates < row_count)
    fetched = shard_piece[jnp.clip(end_dates, 0, row_count - 1)]
    end_tiles = jnp.where(inside[:, None, None, None], fetched, empty_tiles)
    weight, observed = coherence(end_tiles[0::2], end_tiles[1::2])
    weighted = weight * observed
    end_terms = jnp.stack(
        [jnp.stack([weight, -weighted], axis=1), jnp.stack([weight, weighted], axis=1)], axis=1
    )
    end_terms = end_terms.reshape((end_count, 2) + weight.shape[1:])
    targets = jnp.arange(local_dates * lax.axis_size("date"), dtype=jnp.int32)
    one_hot = (end_dates[:, None] == targets[None, :]).astype(jnp.float32)
    assembled = lax.psum_scatter(
        jnp.einsum("ea,eqrc->aqrc", one_hot, end_terms, precision=lax.Precision.HIGHEST),
        "date",
        scatter_dimension=0,
        tiled=True,
    )
    diagonal = DAMPING + assembled[:, 0]
    right_side = assembled[:, 1]
    solution = jnp.zeros_like(right_side)
    residual = right_side
    direction = right_side
    norm_now = squares(residual)
    for step in range(ITERS):
        operator_outgoing = jnp.where(is_valid[:, None, None], direction[local_slot], 0.0)
        operator_incoming = lax.all_to_all(
            operator_outgoing, "date", split_axis=0, concat_axis=0, tiled=True
        )
        end_values = operator_incoming[slot_place]
        coupled = jnp.stack([-weight * end_values[1::2], -weight * end_values[0::2]], axis=1)
        coupled = coupled.reshape((end_count, 1) + weight.shape[1:])
        outgoing = (
            jnp.zeros((date_count * slot_cap,) + coupled.shape[1:], jnp.float32)
            .at[slot_place]
            .set(coupled)
        )
        incoming = lax.all_to_all(outgoing, "date", split_axis=0, concat_axis=0, tiled=True)
        image = (
            diagonal * direction
            + jnp.einsum("ia,iqrc->aqrc", slot_hits, incoming, precision=lax.Precision.HIGHEST)[
                :, 0
            ]
        )
        step_size = norm_now / (curvature(direction, image) + EPSILON)
        solution = solution + step_size * direction
        residual = residual - step_size * image
        if step + 1 < ITERS:
            norm_next = squares(residual)
            direction = residual + norm_next / (norm_now + EPSILON) * direction
            norm_now = norm_next
    return (solution, residual)


def solution(mesh):
    in_specs = (P("date", None, "grp", None), P("date", "grp"), P("date", None), P("date", None))
    out_specs = (P("date", "grp", None), P("date", "grp", None))
    return jax.shard_map(shards, mesh=mesh, in_specs=in_specs, out_specs=out_specs, check_vma=False)
```

profile of v0, /device:TPU:0, one launch (start us, length us, event | category | flops | bytes accessed | tf_op | source)
XLA Modules:
  0.0 479.4 jit_solution(12215435426701859571)
XLA Ops:
  7.2 0.7 convert_element_type.30
  7.9 1.6 broadcast_multiply_fusion
  9.6 0.8 copy.61
  10.5 0.8 copy.62
  11.3 0.7 broadcast_multiply_fusion.1
  12.3 41.0 %all-gather.2.cloned.1.call-done = bf16[96,2,8,512]{3,2,1,0:T(8,128)(2,1)} async-done(((bf16[6,2,8,512]{3,2,1,0:T(8,128)(2,1)}), bf16[96,2,8,512]{3,2,1,0:T(8,128)(2,1)}) %all-gather.2.cloned.1.call-update) | async-done | bytes 1572880 | tf_op jit(solution)/shard_map/all_gather | solution.py:70
  53.3 2.0 gather_fusion
  56.7 0.9 fusion.17
  57.6 3.4 negate_bitcast_fusion
  61.7 2.5 fusion
  64.2 3.5 copy.73
  68.1 0.7 scatter_custom_fusion
  68.9 9.8 %all_to_all.29 = s32[16,5,1]{1,2,0:T(1,128)S(1)} all-to-all(s32[16,5,1]{1,2,0:T(1,128)S(1)} %bitcast.165), channel_id=1, replica_groups=mesh['grp'=2,'date'=16] {'date'}, dimensions={0} | all-to-all | bytes 640 | tf_op jit(solution)/shard_map/all_to_all | solution.py:62
  79.0 54.0 %reduce-scatter.2.cloned.1.call-done = f32[6,2,8,512]{3,2,1,0:T(8,128)} async-done(((f32[96,2,8,512]{3,2,1,0:T(8,128)}), f32[6,2,8,512]{3,2,1,0:T(8,128)}) %reduce-scatter.2.cloned.1.call-update) | async-done | bytes 196624 | tf_op jit(solution)/shard_map/reduce_scatter | solution.py:83
  133.1 1.0 fusion.74
  134.7 1.2 broadcast_select_fusion.2
  135.9 3.9 all-to-all-start.1
  139.8 27.2 %all-to-all-done.1 = f32[80,8,512]{2,1,0:T(8,128)S(1)} async-done(((f32[80,8,512]{2,1,0:T(8,128)}), f32[80,8,512]{2,1,0:T(8,128)S(1)}, u32[]{:S(2)}, u32[]{:S(2)}) %all-to-all-start.1) | async-done | bytes 1310752 | tf_op jit(solution)/shard_map/all_to_all | solution.py:97
  167.9 1.2 broadcast.178.clone
  169.1 8.3 %scatter_fusion = f32[80,8,512]{2,1,0:T(8,128)} fusion(f32[80,8,512]{2,1,0:T(8,128)} %broadcast.178.clone, s32[50]{0:T(128)S(1)} %fusion.66, f32[50,8,512]{2,1,0:T(8,128)S(1)} %bitcast.163), kind=kCustom, calls=%fused_computation.6 | custom fusion | bytes 2457800 | tf_op jit(solution)/shard_map/scatter | solution.py:106
  177.4 8.0 %all-to-all-start.2 = ((f32[80,1,8,512]{3,2,1,0:T(8,128)}), f32[80,1,8,512]{3,2,1,0:T(8,128)S(1)}, u32[]{:S(2)}, u32[]{:S(2)}) async-start(f32[80,1,8,512]{3,2,1,0:T(8,128)} %bitcast.29), calls=%async_computation.3 | async-start | bytes 2621440 | tf_op jit(solution)/shard_map/all_to_all | solution.py:108
  185.5 27.3 %all-to-all-done.2 = f32[80,1,8,512]{3,2,1,0:T(8,128)S(1)} async-done(((f32[80,1,8,512]{3,2,1,0:T(8,128)}), f32[80,1,8,512]{3,2,1,0:T(8,128)S(1)}, u32[]{:S(2)}, u32[]{:S(2)}) %all-to-all-start.2) | async-done | bytes 1310752 | tf_op jit(solution)/shard_map/all_to_all | solution.py:108
  212.8 1.3 fusion.51
  214.1 64.0 %all-reduce.4 = (f32[8,512]{1,0:T(8,128)S(1)}, f32[8,512]{1,0:T(8,128)S(1)}) all-reduce(f32[8,512]{1,0:T(8,128)S(1)} %get-tuple-element.11, f32[8,512]{1,0:T(8,128)S(1)} %get-tuple-element.10), channel_id=1, replica_groups=mesh['grp'=2,'date'=16] {'date'}, use_global_device_ids=true, to_apply=%region_2.3 | all-reduce | flops 8192 | bytes 65536 | tf_op jit(solution)/shard_map/psum | solution.py:40
  278.3 57.6 %psum.30 = f32[8,512]{1,0:T(8,128)S(1)} all-reduce(f32[8,512]{1,0:T(8,128)S(1)} %multiply_reduce_fusion.1), channel_id=1, replica_groups=mesh['grp'=2,'date'=16] {'date'}, use_global_device_ids=true, to_apply=%region_9.10 | all-reduce | flops 4096 | bytes 32768 | tf_op jit(solution)/shard_map/psum | solution.py:40
  336.9 34.1 %all_to_all.30 = f32[80,8,512]{2,1,0:T(8,128)S(1)} all-to-all(f32[80,8,512]{2,1,0:T(8,128)S(1)} %broadcast_select_fusion.1), channel_id=1, replica_groups=mesh['grp'=2,'date'=16] {'date'}, dimensions={0} | all-to-all | bytes 2621440 | tf_op jit(solution)/shard_map/all_to_all | solution.py:97
  372.0 2.5 scatter_fusion.1
  374.6 35.2 %all_to_all.31 = f32[80,1,8,512]{3,2,1,0:T(8,128)S(1)} all-to-all(f32[80,1,8,512]{3,2,1,0:T(8,128)S(1)} %bitcast.160), channel_id=1, replica_groups=mesh['grp'=2,'date'=16] {'date'}, dimensions={0} | all-to-all | bytes 2621440 | tf_op jit(solution)/shard_map/all_to_all | solution.py:108
  409.8 1.3 multiply_reduce_fusion
  411.1 60.0 %psum.31 = f32[8,512]{1,0:T(8,128)S(1)} all-reduce(f32[8,512]{1,0:T(8,128)S(1)} %get-tuple-element.40), channel_id=1, replica_groups=mesh['grp'=2,'date'=16] {'date'}, use_global_device_ids=true, to_apply=%region_12.13 | all-reduce | flops 4096 | bytes 32768 | tf_op jit(solution)/shard_map/psum | solution.py:44
  471.2 0.7 copy.86
  471.9 0.7 copy.87
  (53 shorter events, 7.0 us)
Async XLA Ops:
  7.2 46.1 %all-gather.2.cloned.1.call-start = ((), (), s32[]{:S(2)}) async-start(), calls=%async_computation.6 | async-start | bytes 1671168 | tf_op jit(solution)/shard_map/all_gather | solution.py:70
  9.5 123.5 %reduce-scatter.2.cloned.1.call-start = ((), (), s32[]{:S(2)}) async-start(), calls=%async_computation.7 | async-start | bytes 3342336 | tf_op jit(solution)/shard_map/reduce_scatter | solution.py:83
  135.9 31.1 %all-to-all-start.1 = ((f32[80,8,512]{2,1,0:T(8,128)}), f32[80,8,512]{2,1,0:T(8,128)S(1)}, u32[]{:S(2)}, u32[]{:S(2)}) async-start(f32[80,8,512]{2,1,0:T(8,128)} %broadcast_select_fusion.2), calls=%async_computation.2 | async-start | bytes 2621440 | tf_op jit(solution)/shard_map/all_to_all | solution.py:97
  177.4 35.4 %all-to-all-start.2 = ((f32[80,1,8,512]{3,2,1,0:T(8,128)}), f32[80,1,8,512]{3,2,1,0:T(8,128)S(1)}, u32[]{:S(2)}, u32[]{:S(2)}) async-start(f32[80,1,8,512]{3,2,1,0:T(8,128)} %bitcast.29), calls=%async_computation.3 | async-start | bytes 2621440 | tf_op jit(solution)/shard_map/all_to_all | solution.py:108
Sparse Core Ops, SparseCore 0:
  10.9 42.3 all-gather.1
  67.8 65.1 reduce-scatter.1
where the time goes:
time: 480 us; the launch traced here: 479 us
  blocking collectives  261 us (54%)
  waiting for transfers between devices  150 us (31%)
  local copies, waits for them, and re-layouts  26.3 us (5%)
  between operations  14.4 us (3%)
  starting transfers between devices  12 us (2%)
  other arithmetic  11.4 us (2%)
  matrix products  5.11 us (1%)
    psum x2, blocking collectives, squares(): return lax.psum(jnp.sum(field * field, axis=0), 'date')  122 us
    psum x1, blocking collectives, curvature(): return lax.psum(jnp.sum(direction * image, axis=0), 'date')  60 us
    reduce_scatter x1, waiting for transfers between devices, shards(): lax.psum_scatter(jnp.einsum('ea,eqrc->aqrc', one_hot, end_terms, precisio...  54 us
    all_gather x1, waiting for transfers between devices, shards(): shard_piece = lax.all_gather(masked, 'date', axis=0, tiled=True)  41 us
    all_to_all x1, blocking collectives, shards(): lax.all_to_all(outgoing, 'date', split_axis=0, concat_axis=0, tiled=True)  35.2 us
    all_to_all x1, blocking collectives, shards(): lax.all_to_all(operator_outgoing, 'date', split_axis=0, concat_axis=0, ti...  34.1 us
    all_to_all x1, waiting for transfers between devices, shards(): lax.all_to_all(outgoing, 'date', split_axis=0, concat_axis=0, tiled=True)  27.3 us
    all_to_all x1, waiting for transfers between devices, shards(): lax.all_to_all(operator_outgoing, 'date', split_axis=0, concat_axis=0, ti...  27.2 us
  transfers between devices with their start and end apart: 4, of which 4 were waited for; matrix products, arithmetic and copies ran while one was open for 1% of the time, Pallas kernels for 0%

commit v1 on v0

v1 whole, which is shorter than its diff:
```python
import functools

import jax
import jax.numpy as jnp
from jax import lax
from jax.experimental import pallas as pl
from jax.experimental.pallas import tpu as pltpu
from jax.sharding import PartitionSpec as P

ITERS = 2
DAMPING = 0.5
EPSILON = 1e-06
LANES = 128
HALO = 4
F32 = jnp.float32
BF16 = jnp.bfloat16


def iota(shape, dim):
    return lax.broadcasted_iota(jnp.int32, shape, dim)


def dot(a, b):
    return lax.dot_general(a, b, (((1,), (0,)), ((), ())), preferred_element_type=F32)


def split(x):
    high = x.astype(BF16)
    return high, (x - high.astype(F32)).astype(BF16)


def pack_kernel(mask_ref, dev_ref, slot_ref, slc_ref, out_ref):
    parts = out_ref.shape[0]
    dates, _, rows, cols = slc_ref.shape
    width = cols // parts
    blocks = LANES // width
    tiles = slc_ref[...].astype(F32).reshape(dates * 2 * rows, cols).astype(BF16)
    mask = jnp.concatenate(
        [mask_ref[...].astype(F32), jnp.zeros((8 - dates, rows), F32)], axis=0
    )
    lane = iota((8, dates * 2 * rows), 1)
    row = iota((8, dates * 2 * rows), 0)
    picks = []
    for i in range(rows):
        for c in range(2):
            picks.append(jnp.where(lane == (row * 2 + c) * rows + i, mask[:, i : i + 1], 0.0))
    pick = jnp.concatenate(picks, axis=0).astype(BF16)
    lines = dot(pick, tiles)
    place = iota((cols, 8 * parts), 1)
    j = place % 8
    column = (place // 8) * width + jnp.where(j < HALO, j - HALO, width + j - HALO)
    side = (iota((cols, 8 * parts), 0) == column).astype(F32).astype(BF16)
    edges = dot(lines.astype(BF16), side)

    lane = iota((8, LANES), 1)
    row = iota((8, LANES), 0)
    block = lane // width
    block8 = lane // 8
    pair_count = dev_ref.shape[0]
    pair_lane = iota((pair_count, LANES), 1)
    pair_row = iota((pair_count, LANES), 0)

    def along_lanes(ref):
        value = ref[...].astype(F32)
        total = jnp.zeros((1, LANES), F32)
        for t in range(2):
            hit = pair_lane == pair_row + 64 * t
            total = total + jnp.sum(jnp.where(hit, value[:, t : t + 1], 0.0), axis=0, keepdims=True)
        return total

    index_rows = jnp.where(
        row == 6, along_lanes(dev_ref), jnp.where(row == 7, along_lanes(slot_ref), 0.0)
    )

    def rolled(array, i, c, tile, shift):
        at = (i * 2 + c) * 8
        part = array[at : at + 8, tile * LANES : (tile + 1) * LANES]
        return part if shift % LANES == 0 else pltpu.roll(part, shift % LANES, 1)

    for tile in range(cols // LANES):
        main = {
            (c, h, k): rolled(lines, 4 * h + k, c, tile, width * k)
            for c in range(2)
            for h in range(2)
            for k in range(4)
        }
        for q in range(blocks):
            e = tile * blocks + q
            groups = []
            for c in range(2):
                for h in range(2):
                    total = jnp.zeros((8, LANES), F32)
                    for k in range(4):
                        total = jnp.where(block == (q + k) % blocks, main[c, h, k], total)
                    groups.append(total)
            halo = jnp.zeros((8, LANES), F32)
            for i in range(rows):
                for c in range(2):
                    moved = rolled(edges, i, c, e // 16, 8 * (i + 8 * c))
                    halo = jnp.where(block8 == (e + i + 8 * c) % 16, moved, halo)
            for g in range(3):
                groups[g] = jnp.where(row >= 6, pltpu.roll(halo, 6 - 2 * g, 0), groups[g])
            groups[3] = jnp.where(row >= 6, index_rows, groups[3])
            out_ref[e] = jnp.concatenate(groups, axis=0).astype(BF16)


def strip_kernel(
    dates, pair_count, width, chunk, got_ref, out_ref, first_ref, second_ref, diff_ref, diff_t_ref, weight_ref, term_ref
):
    parts = got_ref.shape[0]
    slots = 8 * parts
    blocks = LANES // width
    pairs = parts * pair_count
    me = lax.axis_index("date")

    got = got_ref[...].astype(F32)
    group = [got[:, 8 * g : 8 * g + 8, :] for g in range(4)]
    row = iota((parts, 8, LANES), 1)
    halo = jnp.where(
        row < 2,
        pltpu.roll(group[0], 2, 1),
        jnp.where(row < 4, pltpu.roll(group[1], 4, 1), pltpu.roll(group[2], 6, 1)),
    )
    columns = [x.reshape(slots, LANES) for x in group + [halo]]
    columns.append(pltpu.roll(columns[4], 64, 1))
    tiles = jnp.concatenate([x.astype(BF16) for x in columns], axis=1)

    at = iota((parts, slots), 1) - 8 * iota((parts, slots), 0)
    take = jnp.where(at == 6, 8.0, jnp.where(at == 7, 1.0, 0.0)).astype(BF16)
    ends = dot(take, columns[3].astype(BF16)).astype(jnp.int32)
    lane = iota((parts, slots), 1)
    for k in range(pair_count):
        first = (ends[:, k : k + 1] == lane).astype(F32)
        second = (ends[:, 64 + k : 65 + k] == lane).astype(F32)
        at = pl.ds(k * parts, parts)
        first_ref[at, :] = first.astype(BF16)
        second_ref[at, :] = second.astype(BF16)
        diff = (second - first).astype(BF16)
        diff_ref[at, :] = jnp.concatenate([diff, diff], axis=1)
    diff_t = jnp.transpose(diff_ref[:, 0:slots].astype(F32)).astype(BF16)
    diff_t_ref[...] = jnp.concatenate([diff_t, diff_t], axis=1)

    def main_place(shape, dim):
        p = iota(shape, dim)
        lane = p % LANES
        k = (lane // width - me + 64) % blocks
        line = jnp.where(k < 4, (p // LANES) * 4 + k, 1000 * (dim + 1))
        return line, lane % width

    def halo_place(shape, dim):
        p = iota(shape, dim)
        t = (p // 8 - me + 64) % 16
        j = p % 8
        return t % 8, jnp.where(j < HALO, j - HALO, width + j - HALO), t // 8

    to_line, to_col = main_place((1, 2 * LANES), 1)
    line, col = main_place((2 * LANES, 1), 0)

    def near(line, col):
        hit = (jnp.abs(line - to_line) <= 1) & (jnp.abs(col - to_col) <= HALO)
        return hit.astype(F32)

    band = near(line, col).astype(BF16)
    line, col, imag = halo_place((LANES, 1), 0)
    band_halo = near(line, col)
    band_cross = (band_halo * (2.0 * imag.astype(F32) - 1.0)).astype(BF16)
    band_halo = band_halo.astype(BF16)
    band_halo = jnp.concatenate([band_halo, band_halo], axis=0)
    band_cross = jnp.concatenate([band_cross, band_cross], axis=0)

    def looks(field, edge, edge_band):
        high, low = split(field)
        edge_high, edge_low = split(edge)
        edges = jnp.concatenate([edge_high, edge_low], axis=1)
        return dot(high, band) + dot(low, band) + dot(edges, edge_band)

    def body(step, carry):
        at = pl.ds(pl.multiple_of(step * chunk, chunk), chunk)
        u = dot(first_ref[at, :], tiles)
        v = dot(second_ref[at, :], tiles)
        u_re, u_im, u_halo = u[:, 0:256], u[:, 256:512], u[:, 512:640]
        v_re, v_im, v_halo, v_swap = v[:, 0:256], v[:, 256:512], v[:, 512:640], v[:, 640:768]
        real = looks(u_re * v_re + u_im * v_im, u_halo * v_halo, band_halo)
        imag = looks(u_im * v_re - u_re * v_im, u_halo * v_swap, band_cross)
        power_ref = looks(u_re * u_re + u_im * u_im, u_halo * u_halo, band_halo)
        power_sec = looks(v_re * v_re + v_im * v_im, v_halo * v_halo, band_halo)
        scale = lax.rsqrt(jnp.maximum(power_ref * power_sec, 1.0))
        real = real * scale
        imag = imag * scale
        weight = real * real + imag * imag
        weight_ref[at, :] = weight
        high, low = split(weight * imag)
        term_ref[at, :] = high
        term_ref[pl.ds(pl.multiple_of(pairs + step * chunk, 16), chunk), :] = low
        return carry

    lax.fori_loop(0, pairs // chunk, body, 0)

    right_side = dot(diff_t_ref[...], term_ref[...])

    def operator(field):
        high, low = split(field)
        spread = dot(diff_ref[...], jnp.concatenate([high, low], axis=0))
        high, low = split(weight_ref[...] * spread)
        term_ref[0:pairs, :] = high
        term_ref[pairs : 2 * pairs, :] = low
        return DAMPING * field + dot(diff_t_ref[...], term_ref[...])

    def inner(a, b):
        return jnp.sum(a * b, axis=0, keepdims=True)

    solution = jnp.zeros_like(right_side)
    residual = right_side
    direction = right_side
    norm_now = inner(residual, residual)
    for step in range(ITERS):
        image = operator(direction)
        step_size = norm_now / (inner(direction, image) + EPSILON)
        solution = solution + step_size * direction
        residual = residual - step_size * image
        if step + 1 < ITERS:
            norm_next = inner(residual, residual)
            direction = residual + norm_next / (norm_now + EPSILON) * direction
            norm_now = norm_next
    for o, field in enumerate((solution, residual)):
        field = field.reshape(parts, 8, 2 * LANES)
        for h in range(2):
            at = (2 * o + h) * dates
            out_ref[:, at : at + dates, :] = field[:, 0:dates, h * LANES : (h + 1) * LANES]


def unpack_kernel(got_ref, *out_refs):
    parts = got_ref.shape[0]
    dates, rows, cols = out_refs[0].shape
    width = cols // parts
    blocks = LANES // width
    block = iota((dates, LANES), 1) // width
    for o, out_ref in enumerate(out_refs):
        for h in range(2):
            at = (2 * o + h) * dates
            for tile in range(cols // LANES):
                for k in range(4):
                    total = jnp.zeros((dates, LANES), F32)
                    for q in range(blocks):
                        part = got_ref[tile * blocks + q, at : at + dates, :]
                        total = jnp.where(block == (q + k) % blocks, part, total)
                    shift = -width * k % LANES
                    if shift:
                        total = pltpu.roll(total, shift, 1)
                    out_ref[:, 4 * h + k, tile * LANES : (tile + 1) * LANES] = total


def shards(slc, line_mask, pair_dev, pair_slot):
    parts = lax.axis_size("date")
    dates, _, rows, cols = slc.shape
    pair_count = pair_dev.shape[0]
    pairs = parts * pair_count
    width = cols // parts
    chunk = max(c for c in range(16, 129, 16) if pairs % c == 0)
    vmem = pl.BlockSpec(memory_space=pltpu.VMEM)

    packed = pl.pallas_call(
        pack_kernel,
        out_shape=jax.ShapeDtypeStruct((parts, 32, LANES), BF16),
        in_specs=[vmem] * 4,
        out_specs=vmem,
        name="pack",
    )(line_mask, pair_dev, pair_slot, slc)
    got = lax.all_to_all(packed, "date", split_axis=0, concat_axis=0, tiled=True)
    fields = pl.pallas_call(
        functools.partial(strip_kernel, dates, pair_count, width, chunk),
        out_shape=jax.ShapeDtypeStruct((parts, 4 * dates, LANES), F32),
        in_specs=[vmem],
        out_specs=vmem,
        scratch_shapes=[
            pltpu.VMEM((pairs, 8 * parts), BF16),
            pltpu.VMEM((pairs, 8 * parts), BF16),
            pltpu.VMEM((pairs, 16 * parts), BF16),
            pltpu.VMEM((8 * parts, 2 * pairs), BF16),
            pltpu.VMEM((pairs, 2 * LANES), F32),
            pltpu.VMEM((2 * pairs, 2 * LANES), BF16),
        ],
        compiler_params=pltpu.CompilerParams(vmem_limit_bytes=48 * 1024 * 1024),
        name="strip",
    )(got)
    back = lax.all_to_all(fields, "date", split_axis=0, concat_axis=0, tiled=True)
    out = jax.ShapeDtypeStruct((dates, rows, cols), F32)
    return pl.pallas_call(
        unpack_kernel,
        out_shape=(out, out),
        in_specs=[vmem],
        out_specs=(vmem, vmem),
        name="unpack",
    )(back)


def solution(mesh):
    in_specs = (P("date", None, "grp", None), P("date", "grp"), P("date", None), P("date", None))
    out_specs = (P("date", "grp", None), P("date", "grp", None))
    return jax.shard_map(shards, mesh=mesh, in_specs=in_specs, out_specs=out_specs, check_vma=False)
```

time: 480 us -> 39.8 us (0.08)
  blocking collectives: 261 us -> 27.6 us
  waiting for transfers between devices: 150 us -> 0 us
  local copies, waits for them, and re-layouts: 26.3 us -> 2.08 us
  between operations: 14.4 us -> 0.65 us
  starting transfers between devices: 12 us -> 0 us
  other arithmetic: 11.4 us -> 0 us
  Pallas kernels: 0 us -> 9.1 us
  matrix products: 5.11 us -> 0 us
    psum x3 -> x0, blocking collectives: 182 us -> none  [the longest x2 122 us: squares(): return lax.psum(jnp.sum(field * field, axis=0), 'date')]
    all_to_all x2 -> x0, waiting for transfers between devices: 54.5 us -> none  [the longest x1 27.3 us: shards(): lax.all_to_all(outgoing, 'date', split_axis=0, concat_axis=0, tiled=True)]
    reduce_scatter x1 -> x0, waiting for transfers between devices: 54 us -> none  [shards(): lax.psum_scatter(jnp.einsum('ea,eqrc->aqrc', one_hot, end_terms, precisio...]
    all_to_all x3 -> x2, blocking collectives: 79.1 us -> 27.6 us  [the longest x1 15.3 us: shards(): lax.all_to_all(packed, 'date', split_axis=0, concat_axis=0, tiled=True)]
    all_gather x1 -> x0, waiting for transfers between devices: 41 us -> none  [shards(): shard_piece = lax.all_gather(masked, 'date', axis=0, tiled=True)]
    all_to_all x2 -> x0, starting transfers between devices: 11.9 us -> none  [the longest x1 8 us: shards(): lax.all_to_all(outgoing, 'date', split_axis=0, concat_axis=0, tiled=True)]
    scatter x3 -> x0, local copies, waits for them, and re-layouts: 11.5 us -> none  [the longest x2 10.8 us: shards(): outgoing = jnp.zeros((date_count * slot_cap,) + coupled.shape[1:], jnp.fl...]
    pallas_call x0 -> x3, Pallas kernels: none -> 9.1 us  [the longest x1 5.27 us: shards(): pl.pallas_call(functools.partial(strip_kernel, dates, pair_count, width,...]
  transfers between devices with their start and end apart: 4 -> 0, of which waited for: 4 -> 0; matrix products, arithmetic and copies ran while one was open for 1% -> 0% of each run, Pallas kernels for 0% -> 0%
where the time goes in v1:
time: 39.8 us; the launch traced here: 39.4 us
  blocking collectives  27.6 us (69%)
  Pallas kernels  9.1 us (23%)
  local copies, waits for them, and re-layouts  2.08 us (5%)
  between operations  0.65 us (2%)
    all_to_all x1, blocking collectives, shards(): lax.all_to_all(packed, 'date', split_axis=0, concat_axis=0, tiled=True)  15.3 us
    all_to_all x1, blocking collectives, shards(): lax.all_to_all(fields, 'date', split_axis=0, concat_axis=0, tiled=True)  12.3 us
    pallas_call x1, Pallas kernels, shards(): pl.pallas_call(functools.partial(strip_kernel, dates, pair_count, width,...  5.27 us
    unnamed x4, local copies, waits for them, and re-layouts  2.08 us
    pallas_call x1, Pallas kernels, shards(): pl.pallas_call(pack_kernel, out_shape=jax.ShapeDtypeStruct((parts, 32, LA...  2.07 us
    pallas_call x1, Pallas kernels, shards(): pl.pallas_call(unpack_kernel, out_shape=(out, out), in_specs=[vmem], out_...  1.76 us

profile of v1, /device:TPU:0, one launch (start us, length us, event | category | flops | bytes accessed | tf_op | source)
XLA Modules:
  0.0 39.4 jit_solution(17054087192014084503)
XLA Ops:
  0.6 0.0 copy-start
  0.6 1.4 %copy.6.dev_ref = s32[25,2]{1,0:T(8,128)} copy(s32[25,2]{0,1:T(2,128)} %param.6) | data formatting | bytes 400 | tf_op args[2]
  2.0 0.0 copy-done
  2.0 0.7 %copy.7.slot_ref = s32[25,2]{1,0:T(8,128)} copy(s32[25,2]{0,1:T(2,128)S(1)} %copy-done) | data formatting | bytes 400 | tf_op args[3]
  2.7 2.1 %pack.1 = bf16[16,32,128]{2,1,0:T(8,128)(2,1)} custom-call(s32[6,8]{1,0:T(8,128)} %mask_ref.1, s32[25,2]{1,0:T(8,128)} %copy.6.dev_ref, s32[25,2]{1,0:T(8,128)} %copy.7.slot_ref, bf16[6,2,8,512]{3,2,1,0:T(8,128)(2,1)} %slc_ref.1), custom_call_target="tpu_custom_call" | custom-call | tf_op jit(solution)/shard_map/pack/pallas_call | solution.py:262
  4.8 15.3 %all_to_all.10.got_ref = bf16[16,32,128]{2,1,0:T(8,128)(2,1)S(1)} all-to-all(bf16[16,32,128]{2,1,0:T(8,128)(2,1)} %pack.1), channel_id=1, replica_groups=mesh['grp'=2,'date'=16] {'date'}, dimensions={0} | all-to-all | bytes 262144 | tf_op jit(solution)/shard_map/all_to_all | solution.py:269
  20.1 5.3 %strip.1 = f32[16,24,128]{2,1,0:T(8,128)S(1)} custom-call(bf16[16,32,128]{2,1,0:T(8,128)(2,1)S(1)} %all_to_all.10.got_ref), custom_call_target="tpu_custom_call" | custom-call | tf_op jit(solution)/shard_map/strip/pallas_call | solution.py:270
  25.4 12.3 %all_to_all.11.got_ref = f32[16,24,128]{2,1,0:T(8,128)} all-to-all(f32[16,24,128]{2,1,0:T(8,128)S(1)} %strip.1), channel_id=1, replica_groups=mesh['grp'=2,'date'=16] {'date'}, dimensions={0} | all-to-all | bytes 393216 | tf_op jit(solution)/shard_map/all_to_all | solution.py:286
  37.7 1.8 %unpack.1 = (f32[6,8,512]{2,1,0:T(8,128)}, f32[6,8,512]{2,1,0:T(8,128)}) custom-call(f32[16,24,128]{2,1,0:T(8,128)} %all_to_all.11.got_ref), custom_call_target="tpu_custom_call" | custom-call | tf_op jit(solution)/shard_map/unpack/pallas_call | solution.py:288
Async XLA Ops:
  0.6 1.4 %copy-start = (s32[25,2]{0,1:T(2,128)S(1)}, s32[25,2]{0,1:T(2,128)}, u32[]{:S(2)}) copy-start(s32[25,2]{0,1:T(2,128)} %param.7) | copy-start | bytes 604

commit v2 on v1

--- a/solution.py
+++ b/solution.py
@@ -56,21 +56,12 @@
     row = iota((8, LANES), 0)
     block = lane // width
     block8 = lane // 8
-    pair_count = dev_ref.shape[0]
-    pair_lane = iota((pair_count, LANES), 1)
-    pair_row = iota((pair_count, LANES), 0)
-
-    def along_lanes(ref):
-        value = ref[...].astype(F32)
-        total = jnp.zeros((1, LANES), F32)
-        for t in range(2):
-            hit = pair_lane == pair_row + 64 * t
-            total = total + jnp.sum(jnp.where(hit, value[:, t : t + 1], 0.0), axis=0, keepdims=True)
-        return total
-
-    index_rows = jnp.where(
-        row == 6, along_lanes(dev_ref), jnp.where(row == 7, along_lanes(slot_ref), 0.0)
+    pair_count = dev_ref.shape[1]
+    spare = jnp.zeros((2, 64 - pair_count), F32)
+    index_rows = jnp.concatenate(
+        [dev_ref[...].astype(F32), spare, slot_ref[...].astype(F32), spare], axis=1
     )
+    index_rows = jnp.concatenate([jnp.zeros((6, LANES), F32), index_rows], axis=0)
 
     def rolled(array, i, c, tile, shift):
         at = (i * 2 + c) * 8
@@ -125,13 +116,14 @@
     columns.append(pltpu.roll(columns[4], 64, 1))
     tiles = jnp.concatenate([x.astype(BF16) for x in columns], axis=1)
 
-    at = iota((parts, slots), 1) - 8 * iota((parts, slots), 0)
-    take = jnp.where(at == 6, 8.0, jnp.where(at == 7, 1.0, 0.0)).astype(BF16)
-    ends = dot(take, columns[3].astype(BF16)).astype(jnp.int32)
+    at = iota((2 * parts, slots), 1) - 8 * (iota((2 * parts, slots), 0) % parts)
+    take = (at == 6 + iota((2 * parts, slots), 0) // parts).astype(F32).astype(BF16)
+    ends = dot(take, columns[3].astype(BF16))
+    ends = (8.0 * ends + pltpu.roll(ends, 64, 1)).astype(jnp.int32)
     lane = iota((parts, slots), 1)
     for k in range(pair_count):
-        first = (ends[:, k : k + 1] == lane).astype(F32)
-        second = (ends[:, 64 + k : 65 + k] == lane).astype(F32)
+        first = (ends[0:parts, k : k + 1] == lane).astype(F32)
+        second = (ends[parts : 2 * parts, k : k + 1] == lane).astype(F32)
         at = pl.ds(k * parts, parts)
         first_ref[at, :] = first.astype(BF16)
         second_ref[at, :] = second.astype(BF16)
@@ -264,8 +256,9 @@
         out_shape=jax.ShapeDtypeStruct((parts, 32, LANES), BF16),
         in_specs=[vmem] * 4,
         out_specs=vmem,
+        compiler_params=pltpu.CompilerParams(vmem_limit_bytes=4 * 1024 * 1024),
         name="pack",
-    )(line_mask, pair_dev, pair_slot, slc)
+    )(line_mask, pair_dev.T, pair_slot.T, slc)
     got = lax.all_to_all(packed, "date", split_axis=0, concat_axis=0, tiled=True)
     fields = pl.pallas_call(
         functools.partial(strip_kernel, dates, pair_count, width, chunk),
@@ -280,7 +273,7 @@
             pltpu.VMEM((pairs, 2 * LANES), F32),
             pltpu.VMEM((2 * pairs, 2 * LANES), BF16),
         ],
-        compiler_params=pltpu.CompilerParams(vmem_limit_bytes=48 * 1024 * 1024),
+        compiler_params=pltpu.CompilerParams(vmem_limit_bytes=24 * 1024 * 1024),
         name="strip",
     )(got)
     back = lax.all_to_all(fields, "date", split_axis=0, concat_axis=0, tiled=True)
@@ -290,6 +283,7 @@
         out_shape=(out, out),
         in_specs=[vmem],
         out_specs=(vmem, vmem),
+        compiler_params=pltpu.CompilerParams(vmem_limit_bytes=4 * 1024 * 1024),
         name="unpack",
     )(back)
 

time: 39.8 us -> 36.6 us (0.920)
  Pallas kernels: 9.1 us -> 6.69 us
  blocking collectives: 27.6 us -> 26.7 us
    pallas_call x1, Pallas kernels: 2.07 us -> 0.47 us  [shards(): pl.pallas_call(pack_kernel, out_shape=jax.ShapeDtypeStruct((parts, 32, LA...]
    pallas_call x1, Pallas kernels: 1.76 us -> 0.83 us  [shards(): pl.pallas_call(unpack_kernel, out_shape=(out, out), in_specs=[vmem], out_...]
    all_to_all x1, blocking collectives: 12.3 us -> 11.6 us  [shards(): lax.all_to_all(fields, 'date', split_axis=0, concat_axis=0, tiled=True)]
    unnamed x4 -> x8, local copies, waits for them, and re-layouts: 2.08 us -> 2.26 us
where the time goes in v2:
time: 36.6 us; the launch traced here: 36.3 us
  blocking collectives  26.7 us (73%)
  Pallas kernels  6.69 us (18%)
  local copies, waits for them, and re-layouts  2.26 us (6%)
  between operations  0.67 us (2%)
    all_to_all x1, blocking collectives, shards(): lax.all_to_all(packed, 'date', split_axis=0, concat_axis=0, tiled=True)  15.1 us
    all_to_all x1, blocking collectives, shards(): lax.all_to_all(fields, 'date', split_axis=0, concat_axis=0, tiled=True)  11.6 us
    pallas_call x1, Pallas kernels, shards(): pl.pallas_call(functools.partial(strip_kernel, dates, pair_count, width,...  5.39 us
    unnamed x8, local copies, waits for them, and re-layouts  2.26 us
    pallas_call x1, Pallas kernels, shards(): pl.pallas_call(unpack_kernel, out_shape=(out, out), in_specs=[vmem], out_...  0.83 us

profile of v2, /device:TPU:0, one launch (start us, length us, event | category | flops | bytes accessed | tf_op | source)
XLA Modules:
  0.0 36.3 jit_solution(2577250798804683424)
XLA Ops:
  0.6 0.0 copy-start.3
  0.6 0.0 copy-start.2
  0.7 0.7 %copy-done.3 = s32[25,2]{0,1:T(2,128)S(1)} copy-done((s32[25,2]{0,1:T(2,128)S(1)}, s32[25,2]{0,1:T(2,128)}, u32[]{:S(2)}) %copy-start.3) | copy-done | bytes 224
  1.3 0.0 copy-done.2
  1.3 0.0 copy-start
  1.3 0.9 %copy-done = bf16[6,2,8,512]{3,2,1,0:T(8,128)(2,1)S(1)} copy-done((bf16[6,2,8,512]{3,2,1,0:T(8,128)(2,1)S(1)}, bf16[6,2,8,512]{3,2,1,0:T(8,128)(2,1)}, u32[]{:S(2)}) %copy-start) | copy-done | bytes 98328
  2.2 0.0 copy-start.1
  2.2 0.7 %copy-done.1 = s32[6,8]{1,0:T(8,128)S(1)} copy-done((s32[6,8]{1,0:T(8,128)S(1)}, s32[6,8]{1,0:T(8,128)}, u32[]{:S(2)}) %copy-start.1) | copy-done | bytes 216
  2.9 0.5 %pack.1 = bf16[16,32,128]{2,1,0:T(8,128)(2,1)S(1)} custom-call(s32[6,8]{1,0:T(8,128)S(1)} %copy-done.1, s32[2,25]{1,0:T(2,128)S(1)} %bitcast.2, s32[2,25]{1,0:T(2,128)S(1)} %bitcast.3, bf16[6,2,8,512]{3,2,1,0:T(8,128)(2,1)S(1)} %copy-done), custom_call_target="tpu_custom_call" | custom-call | tf_op jit(solution)/shard_map/pack/pallas_call | solution.py:254
  3.4 15.1 %all_to_all.10.got_ref = bf16[16,32,128]{2,1,0:T(8,128)(2,1)S(1)} all-to-all(bf16[16,32,128]{2,1,0:T(8,128)(2,1)S(1)} %pack.1), channel_id=1, replica_groups=mesh['grp'=2,'date'=16] {'date'}, dimensions={0} | all-to-all | bytes 262144 | tf_op jit(solution)/shard_map/all_to_all | solution.py:262
  18.5 5.4 %strip.1 = f32[16,24,128]{2,1,0:T(8,128)S(1)} custom-call(bf16[16,32,128]{2,1,0:T(8,128)(2,1)S(1)} %all_to_all.10.got_ref), custom_call_target="tpu_custom_call" | custom-call | tf_op jit(solution)/shard_map/strip/pallas_call | solution.py:263
  23.9 11.6 %all_to_all.11.got_ref = f32[16,24,128]{2,1,0:T(8,128)S(1)} all-to-all(f32[16,24,128]{2,1,0:T(8,128)S(1)} %strip.1), channel_id=1, replica_groups=mesh['grp'=2,'date'=16] {'date'}, dimensions={0} | all-to-all | bytes 393216 | tf_op jit(solution)/shard_map/all_to_all | solution.py:279
  35.5 0.8 %unpack.1 = (f32[6,8,512]{2,1,0:T(8,128)}, f32[6,8,512]{2,1,0:T(8,128)}) custom-call(f32[16,24,128]{2,1,0:T(8,128)S(1)} %all_to_all.11.got_ref), custom_call_target="tpu_custom_call" | custom-call | tf_op jit(solution)/shard_map/unpack/pallas_call | solution.py:281
Async XLA Ops:
  0.6 0.7 %copy-start.3 = (s32[25,2]{0,1:T(2,128)S(1)}, s32[25,2]{0,1:T(2,128)}, u32[]{:S(2)}) copy-start(s32[25,2]{0,1:T(2,128)} %param.7) | copy-start | bytes 604
  0.6 0.7 %copy-start.2 = (s32[25,2]{0,1:T(2,128)S(1)}, s32[25,2]{0,1:T(2,128)}, u32[]{:S(2)}) copy-start(s32[25,2]{0,1:T(2,128)} %param.6) | copy-start | bytes 604
  1.3 0.9 %copy-start = (bf16[6,2,8,512]{3,2,1,0:T(8,128)(2,1)S(1)}, bf16[6,2,8,512]{3,2,1,0:T(8,128)(2,1)}, u32[]{:S(2)}) copy-start(bf16[6,2,8,512]{3,2,1,0:T(8,128)(2,1)} %slc_ref.1) | copy-start | bytes 294916
  2.2 0.7 %copy-start.1 = (s32[6,8]{1,0:T(8,128)S(1)}, s32[6,8]{1,0:T(8,128)}, u32[]{:S(2)}) copy-start(s32[6,8]{1,0:T(8,128)} %mask_ref.1) | copy-start | bytes 580

commit v3 on v2

--- a/solution.py
+++ b/solution.py
@@ -29,7 +29,17 @@
     return high, (x - high.astype(F32)).astype(BF16)
 
 
-def pack_kernel(mask_ref, dev_ref, slot_ref, slc_ref, out_ref):
+def pack_kernel(mask_in, dev_in, slot_in, slc_in, out_ref, mask_ref, dev_ref, slot_ref, slc_ref, sems):
+    copies = [
+        pltpu.make_async_copy(source, target, sems.at[n])
+        for n, (source, target) in enumerate(
+            ((slc_in, slc_ref), (mask_in, mask_ref), (dev_in, dev_ref), (slot_in, slot_ref))
+        )
+    ]
+    for copy in copies:
+        copy.start()
+    for copy in copies:
+        copy.wait()
     parts = out_ref.shape[0]
     dates, _, rows, cols = slc_ref.shape
     width = cols // parts
@@ -113,8 +123,6 @@
         jnp.where(row < 4, pltpu.roll(group[1], 4, 1), pltpu.roll(group[2], 6, 1)),
     )
     columns = [x.reshape(slots, LANES) for x in group + [halo]]
-    columns.append(pltpu.roll(columns[4], 64, 1))
-    tiles = jnp.concatenate([x.astype(BF16) for x in columns], axis=1)
 
     at = iota((2 * parts, slots), 1) - 8 * (iota((2 * parts, slots), 0) % parts)
     take = (at == 6 + iota((2 * parts, slots), 0) // parts).astype(F32).astype(BF16)
@@ -125,10 +133,9 @@
         first = (ends[0:parts, k : k + 1] == lane).astype(F32)
         second = (ends[parts : 2 * parts, k : k + 1] == lane).astype(F32)
         at = pl.ds(k * parts, parts)
-        first_ref[at, :] = first.astype(BF16)
-        second_ref[at, :] = second.astype(BF16)
-        diff = (second - first).astype(BF16)
-        diff_ref[at, :] = jnp.concatenate([diff, diff], axis=1)
+        for ref, value in ((first_ref, first), (second_ref, second), (diff_ref, second - first)):
+            value = value.astype(BF16)
+            ref[at, :] = jnp.concatenate([value, value], axis=1)
     diff_t = jnp.transpose(diff_ref[:, 0:slots].astype(F32)).astype(BF16)
     diff_t_ref[...] = jnp.concatenate([diff_t, diff_t], axis=1)
 
@@ -146,37 +153,52 @@
         return t % 8, jnp.where(j < HALO, j - HALO, width + j - HALO), t // 8
 
     to_line, to_col = main_place((1, 2 * LANES), 1)
-    line, col = main_place((2 * LANES, 1), 0)
 
     def near(line, col):
         hit = (jnp.abs(line - to_line) <= 1) & (jnp.abs(col - to_col) <= HALO)
         return hit.astype(F32)
 
-    band = near(line, col).astype(BF16)
+    band = near(*main_place((2 * LANES, 1), 0)).astype(BF16)
     line, col, imag = halo_place((LANES, 1), 0)
     band_halo = near(line, col)
     band_cross = (band_halo * (2.0 * imag.astype(F32) - 1.0)).astype(BF16)
     band_halo = band_halo.astype(BF16)
-    band_halo = jnp.concatenate([band_halo, band_halo], axis=0)
-    band_cross = jnp.concatenate([band_cross, band_cross], axis=0)
-
-    def looks(field, edge, edge_band):
-        high, low = split(field)
-        edge_high, edge_low = split(edge)
-        edges = jnp.concatenate([edge_high, edge_low], axis=1)
-        return dot(high, band) + dot(low, band) + dot(edges, edge_band)
+    band_halo = jnp.concatenate([band, band, band_halo, band_halo], axis=0)
+    band_cross = jnp.concatenate([band, band, band_cross, band_cross], axis=0)
+
+    def looks(field, edge, table):
+        return dot(jnp.concatenate([*split(field), *split(edge)], axis=1), table)
+
+    re = jnp.concatenate(columns[0:2], axis=1)
+    im = jnp.concatenate(columns[2:4], axis=1)
+    power_high, power_low = split(looks(re * re + im * im, columns[4] * columns[4], band_halo))
+    tiles = jnp.concatenate([x.astype(BF16) for x in columns], axis=1)
+    swap = pltpu.roll(columns[4], 64, 1).astype(BF16)
+    zero = jnp.zeros_like(tiles)
+    first_tiles = jnp.concatenate(
+        [
+            jnp.concatenate([power_high, tiles], axis=1),
+            jnp.concatenate([power_low, zero], axis=1),
+        ],
+        axis=0,
+    )
+    second_tiles = jnp.concatenate(
+        [
+            jnp.concatenate([power_high, tiles, swap], axis=1),
+            jnp.concatenate([power_low, zero, jnp.zeros_like(swap)], axis=1),
+        ],
+        axis=0,
+    )
 
     def body(step, carry):
-        at = pl.ds(pl.multiple_of(step * chunk, chunk), chunk)
-        u = dot(first_ref[at, :], tiles)
-        v = dot(second_ref[at, :], tiles)
-        u_re, u_im, u_halo = u[:, 0:256], u[:, 256:512], u[:, 512:640]
-        v_re, v_im, v_halo, v_swap = v[:, 0:256], v[:, 256:512], v[:, 512:640], v[:, 640:768]
+        at = pl.ds(pl.multiple_of(step * chunk, 16), chunk)
+        u = dot(first_ref[at, :], first_tiles)
+        v = dot(second_ref[at, :], second_tiles)
+        u_power, u_re, u_im, u_halo = u[:, 0:256], u[:, 256:512], u[:, 512:768], u[:, 768:896]
+        v_power, v_re, v_im, v_halo = v[:, 0:256], v[:, 256:512], v[:, 512:768], v[:, 768:896]
         real = looks(u_re * v_re + u_im * v_im, u_halo * v_halo, band_halo)
-        imag = looks(u_im * v_re - u_re * v_im, u_halo * v_swap, band_cross)
-        power_ref = looks(u_re * u_re + u_im * u_im, u_halo * u_halo, band_halo)
-        power_sec = looks(v_re * v_re + v_im * v_im, v_halo * v_halo, band_halo)
-        scale = lax.rsqrt(jnp.maximum(power_ref * power_sec, 1.0))
+        imag = looks(u_im * v_re - u_re * v_im, u_halo * v[:, 896:1024], band_cross)
+        scale = lax.rsqrt(jnp.maximum(u_power * v_power, 1.0))
         real = real * scale
         imag = imag * scale
         weight = real * real + imag * imag
@@ -186,7 +208,10 @@
         term_ref[pl.ds(pl.multiple_of(pairs + step * chunk, 16), chunk), :] = low
         return carry
 
-    lax.fori_loop(0, pairs // chunk, body, 0)
+    if chunk == pairs:
+        body(0, 0)
+    else:
+        lax.fori_loop(0, pairs // chunk, body, 0)
 
     right_side = dot(diff_t_ref[...], term_ref[...])
 
@@ -248,17 +273,29 @@
     pair_count = pair_dev.shape[0]
     pairs = parts * pair_count
     width = cols // parts
-    chunk = max(c for c in range(16, 129, 16) if pairs % c == 0)
+    chunk = max(c for c in range(16, 513, 16) if pairs % c == 0)
     vmem = pl.BlockSpec(memory_space=pltpu.VMEM)
 
     packed = pl.pallas_call(
         pack_kernel,
         out_shape=jax.ShapeDtypeStruct((parts, 32, LANES), BF16),
-        in_specs=[vmem] * 4,
+        in_specs=[pl.BlockSpec(memory_space=pltpu.HBM)] * 4,
         out_specs=vmem,
+        scratch_shapes=[
+            pltpu.VMEM((dates, rows), jnp.int32),
+            pltpu.VMEM((2, pair_count), jnp.int32),
+            pltpu.VMEM((2, pair_count), jnp.int32),
+            pltpu.VMEM(slc.shape, BF16),
+            pltpu.SemaphoreType.DMA((4,)),
+        ],
         compiler_params=pltpu.CompilerParams(vmem_limit_bytes=4 * 1024 * 1024),
         name="pack",
-    )(line_mask, pair_dev.T, pair_slot.T, slc)
+    )(
+        *[
+            pltpu.with_memory_space_constraint(x, pltpu.HBM)
+            for x in (line_mask, pair_dev.T, pair_slot.T, slc)
+        ]
+    )
     got = lax.all_to_all(packed, "date", split_axis=0, concat_axis=0, tiled=True)
     fields = pl.pallas_call(
         functools.partial(strip_kernel, dates, pair_count, width, chunk),
@@ -266,8 +303,8 @@
         in_specs=[vmem],
         out_specs=vmem,
         scratch_shapes=[
-            pltpu.VMEM((pairs, 8 * parts), BF16),
-            pltpu.VMEM((pairs, 8 * parts), BF16),
+            pltpu.VMEM((pairs, 16 * parts), BF16),
+            pltpu.VMEM((pairs, 16 * parts), BF16),
             pltpu.VMEM((pairs, 16 * parts), BF16),
             pltpu.VMEM((8 * parts, 2 * pairs), BF16),
             pltpu.VMEM((pairs, 2 * LANES), F32),

time: 36.6 us -> 32.7 us (0.89)
  local copies, waits for them, and re-layouts: 2.26 us -> 0 us
  Pallas kernels: 6.69 us -> 5.08 us
    pallas_call x1, Pallas kernels: 5.39 us -> 2.84 us  [shards(): pl.pallas_call(functools.partial(strip_kernel, dates, pair_count, width,...]
    unnamed x8 -> x0, local copies, waits for them, and re-layouts: 2.26 us -> none
    pallas_call x1, Pallas kernels: 0.47 us -> 1.4 us  [shards(): pl.pallas_call(pack_kernel, out_shape=jax.ShapeDtypeStruct((parts, 32, LA...]
where the time goes in v3:
time: 32.7 us; the launch traced here: 32.4 us
  blocking collectives  26.7 us (82%)
  Pallas kernels  5.08 us (16%)
  between operations  0.65 us (2%)
    all_to_all x1, blocking collectives, shards(): lax.all_to_all(packed, 'date', split_axis=0, concat_axis=0, tiled=True)  15.1 us
    all_to_all x1, blocking collectives, shards(): lax.all_to_all(fields, 'date', split_axis=0, concat_axis=0, tiled=True)  11.6 us
    pallas_call x1, Pallas kernels, shards(): pl.pallas_call(functools.partial(strip_kernel, dates, pair_count, width,...  2.84 us
    pallas_call x1, Pallas kernels, shards(): pl.pallas_call(pack_kernel, out_shape=jax.ShapeDtypeStruct((parts, 32, LA...  1.4 us
    pallas_call x1, Pallas kernels, shards(): pl.pallas_call(unpack_kernel, out_shape=(out, out), in_specs=[vmem], out_...  0.83 us

profile of v3, /device:TPU:0, one launch (start us, length us, event | category | flops | bytes accessed | tf_op | source)
XLA Modules:
  0.0 32.4 jit_solution(4439387699152296826)
XLA Ops:
  0.6 1.4 %pack.1 = bf16[16,32,128]{2,1,0:T(8,128)(2,1)S(1)} custom-call(s32[6,8]{1,0:T(8,128)} %mask_in.1, s32[2,25]{1,0:T(2,128)} %bitcast.2, s32[2,25]{1,0:T(2,128)} %bitcast.3, bf16[6,2,8,512]{3,2,1,0:T(8,128)(2,1)} %slc_in.1), custom_call_target="tpu_custom_call" | custom-call | tf_op jit(solution)/shard_map/pack/pallas_call | solution.py:279
  2.0 15.1 %all_to_all.10.got_ref = bf16[16,32,128]{2,1,0:T(8,128)(2,1)S(1)} all-to-all(bf16[16,32,128]{2,1,0:T(8,128)(2,1)S(1)} %pack.1), channel_id=1, replica_groups=mesh['grp'=2,'date'=16] {'date'}, dimensions={0} | all-to-all | bytes 262144 | tf_op jit(solution)/shard_map/all_to_all | solution.py:299
  17.2 2.8 %strip.1 = f32[16,24,128]{2,1,0:T(8,128)S(1)} custom-call(bf16[16,32,128]{2,1,0:T(8,128)(2,1)S(1)} %all_to_all.10.got_ref), custom_call_target="tpu_custom_call" | custom-call | tf_op jit(solution)/shard_map/strip/pallas_call | solution.py:300
  20.0 11.6 %all_to_all.11.got_ref = f32[16,24,128]{2,1,0:T(8,128)S(1)} all-to-all(f32[16,24,128]{2,1,0:T(8,128)S(1)} %strip.1), channel_id=1, replica_groups=mesh['grp'=2,'date'=16] {'date'}, dimensions={0} | all-to-all | bytes 393216 | tf_op jit(solution)/shard_map/all_to_all | solution.py:316
  31.6 0.8 %unpack.1 = (f32[6,8,512]{2,1,0:T(8,128)}, f32[6,8,512]{2,1,0:T(8,128)}) custom-call(f32[16,24,128]{2,1,0:T(8,128)S(1)} %all_to_all.11.got_ref), custom_call_target="tpu_custom_call" | custom-call | tf_op jit(solution)/shard_map/unpack/pallas_call | solution.py:318

commit v4 on v3

--- a/solution.py
+++ b/solution.py
@@ -29,22 +29,30 @@
     return high, (x - high.astype(F32)).astype(BF16)
 
 
-def pack_kernel(mask_in, dev_in, slot_in, slc_in, out_ref, mask_ref, dev_ref, slot_ref, slc_ref, sems):
+def pack_kernel(mask_in, dev_in, slot_in, slc_in, out_ref, mask_ref, dev_ref, slot_ref, slc_ref, side_ref, sems):
+    step = slc_ref.shape[0] // 3
     copies = [
         pltpu.make_async_copy(source, target, sems.at[n])
         for n, (source, target) in enumerate(
-            ((slc_in, slc_ref), (mask_in, mask_ref), (dev_in, dev_ref), (slot_in, slot_ref))
+            [(mask_in, mask_ref), (dev_in, dev_ref), (slot_in, slot_ref)]
+            + [
+                (slc_in.at[pl.ds(a, step)], slc_ref.at[pl.ds(a, step)])
+                for a in range(0, slc_ref.shape[0], step)
+            ]
         )
     ]
     for copy in copies:
         copy.start()
-    for copy in copies:
-        copy.wait()
     parts = out_ref.shape[0]
     dates, _, rows, cols = slc_ref.shape
     width = cols // parts
     blocks = LANES // width
-    tiles = slc_ref[...].astype(F32).reshape(dates * 2 * rows, cols).astype(BF16)
+    place = iota((cols, 8 * parts), 1)
+    j = place % 8
+    column = (place // 8) * width + jnp.where(j < HALO, j - HALO, width + j - HALO)
+    side_ref[...] = (iota((cols, 8 * parts), 0) == column).astype(F32).astype(BF16)
+    for copy in copies[:3]:
+        copy.wait()
     mask = jnp.concatenate(
         [mask_ref[...].astype(F32), jnp.zeros((8 - dates, rows), F32)], axis=0
     )
@@ -55,12 +63,11 @@
         for c in range(2):
             picks.append(jnp.where(lane == (row * 2 + c) * rows + i, mask[:, i : i + 1], 0.0))
     pick = jnp.concatenate(picks, axis=0).astype(BF16)
+    for copy in copies[3:]:
+        copy.wait()
+    tiles = slc_ref[...].astype(F32).reshape(dates * 2 * rows, cols).astype(BF16)
     lines = dot(pick, tiles)
-    place = iota((cols, 8 * parts), 1)
-    j = place % 8
-    column = (place // 8) * width + jnp.where(j < HALO, j - HALO, width + j - HALO)
-    side = (iota((cols, 8 * parts), 0) == column).astype(F32).astype(BF16)
-    edges = dot(lines.astype(BF16), side)
+    edges = dot(lines.astype(BF16), side_ref[...])
 
     lane = iota((8, LANES), 1)
     row = iota((8, LANES), 0)
@@ -239,11 +246,18 @@
             norm_next = inner(residual, residual)
             direction = residual + norm_next / (norm_now + EPSILON) * direction
             norm_now = norm_next
-    for o, field in enumerate((solution, residual)):
+    row = iota((parts, 8, LANES), 1)
+    groups = []
+    for field in (solution, residual):
         field = field.reshape(parts, 8, 2 * LANES)
         for h in range(2):
-            at = (2 * o + h) * dates
-            out_ref[:, at : at + dates, :] = field[:, 0:dates, h * LANES : (h + 1) * LANES]
+            part = field[:, :, h * LANES : (h + 1) * LANES]
+            largest = jnp.max(jnp.abs(part), axis=1, keepdims=True)
+            power = jnp.floor(jnp.log2(jnp.maximum(largest, 2.0**-126))) + 1.0
+            coded = jnp.floor(part * jnp.exp2(-power) * 32768.0 + 0.5)
+            coded = jnp.where(row == 6, power, jnp.clip(coded, -32767.0, 32767.0))
+            groups.append(coded.astype(jnp.int32))
+    out_ref[...] = jnp.concatenate(groups, axis=1).astype(jnp.int16)
 
 
 def unpack_kernel(got_ref, *out_refs):
@@ -251,20 +265,21 @@
     dates, rows, cols = out_refs[0].shape
     width = cols // parts
     blocks = LANES // width
-    block = iota((dates, LANES), 1) // width
+    block = iota((8, LANES), 1) // width
+    got = got_ref[...].astype(jnp.int32).astype(F32)
     for o, out_ref in enumerate(out_refs):
         for h in range(2):
-            at = (2 * o + h) * dates
+            at = (2 * o + h) * 8
+            part = got[:, at : at + 8, :] * 2.0**-15 * jnp.exp2(got[:, at + 6 : at + 7, :])
             for tile in range(cols // LANES):
                 for k in range(4):
-                    total = jnp.zeros((dates, LANES), F32)
+                    total = jnp.zeros((8, LANES), F32)
                     for q in range(blocks):
-                        part = got_ref[tile * blocks + q, at : at + dates, :]
-                        total = jnp.where(block == (q + k) % blocks, part, total)
+                        total = jnp.where(block == (q + k) % blocks, part[tile * blocks + q], total)
                     shift = -width * k % LANES
                     if shift:
                         total = pltpu.roll(total, shift, 1)
-                    out_ref[:, 4 * h + k, tile * LANES : (tile + 1) * LANES] = total
+                    out_ref[:, 4 * h + k, tile * LANES : (tile + 1) * LANES] = total[0:dates]
 
 
 def shards(slc, line_mask, pair_dev, pair_slot):
@@ -286,7 +301,8 @@
             pltpu.VMEM((2, pair_count), jnp.int32),
             pltpu.VMEM((2, pair_count), jnp.int32),
             pltpu.VMEM(slc.shape, BF16),
-            pltpu.SemaphoreType.DMA((4,)),
+            pltpu.VMEM((cols, 8 * parts), BF16),
+            pltpu.SemaphoreType.DMA((6,)),
         ],
         compiler_params=pltpu.CompilerParams(vmem_limit_bytes=4 * 1024 * 1024),
         name="pack",
@@ -299,7 +315,7 @@
     got = lax.all_to_all(packed, "date", split_axis=0, concat_axis=0, tiled=True)
     fields = pl.pallas_call(
         functools.partial(strip_kernel, dates, pair_count, width, chunk),
-        out_shape=jax.ShapeDtypeStruct((parts, 4 * dates, LANES), F32),
+        out_shape=jax.ShapeDtypeStruct((parts, 32, LANES), jnp.int16),
         in_specs=[vmem],
         out_specs=vmem,
         scratch_shapes=[

time: 32.7 us -> 31.8 us (0.972)
  blocking collectives: 26.7 us -> 25.6 us
    all_to_all x1, blocking collectives: 11.6 us -> 10.5 us  [shards(): lax.all_to_all(fields, 'date', split_axis=0, concat_axis=0, tiled=True)]
where the time goes in v4:
time: 31.8 us; the launch traced here: 31.5 us
  blocking collectives  25.6 us (81%)
  Pallas kernels  5.19 us (16%)
  between operations  0.65 us (2%)
    all_to_all x1, blocking collectives, shards(): lax.all_to_all(packed, 'date', split_axis=0, concat_axis=0, tiled=True)  15.1 us
    all_to_all x1, blocking collectives, shards(): lax.all_to_all(fields, 'date', split_axis=0, concat_axis=0, tiled=True)  10.5 us
    pallas_call x1, Pallas kernels, shards(): pl.pallas_call(functools.partial(strip_kernel, dates, pair_count, width,...  3.04 us
    pallas_call x1, Pallas kernels, shards(): pl.pallas_call(pack_kernel, out_shape=jax.ShapeDtypeStruct((parts, 32, LA...  1.3 us
    pallas_call x1, Pallas kernels, shards(): pl.pallas_call(unpack_kernel, out_shape=(out, out), in_specs=[vmem], out_...  0.85 us

profile of v4, /device:TPU:0, one launch (start us, length us, event | category | flops | bytes accessed | tf_op | source)
XLA Modules:
  0.0 31.5 jit_solution(5395489504828589903)
XLA Ops:
  0.6 1.3 %pack.1 = bf16[16,32,128]{2,1,0:T(8,128)(2,1)S(1)} custom-call(s32[6,8]{1,0:T(8,128)} %mask_in.1, s32[2,25]{1,0:T(2,128)} %bitcast.2, s32[2,25]{1,0:T(2,128)} %bitcast.3, bf16[6,2,8,512]{3,2,1,0:T(8,128)(2,1)} %slc_in.1), custom_call_target="tpu_custom_call" | custom-call | tf_op jit(solution)/shard_map/pack/pallas_call | solution.py:294
  1.9 15.1 %all_to_all.10.got_ref = bf16[16,32,128]{2,1,0:T(8,128)(2,1)S(1)} all-to-all(bf16[16,32,128]{2,1,0:T(8,128)(2,1)S(1)} %pack.1), channel_id=1, replica_groups=mesh['grp'=2,'date'=16] {'date'}, dimensions={0} | all-to-all | bytes 262144 | tf_op jit(solution)/shard_map/all_to_all | solution.py:315
  17.1 3.0 %strip.1 = s16[16,32,128]{2,1,0:T(8,128)(2,1)S(1)} custom-call(bf16[16,32,128]{2,1,0:T(8,128)(2,1)S(1)} %all_to_all.10.got_ref), custom_call_target="tpu_custom_call" | custom-call | tf_op jit(solution)/shard_map/strip/pallas_call | solution.py:316
  20.1 10.5 %all_to_all.11.got_ref = s16[16,32,128]{2,1,0:T(8,128)(2,1)S(1)} all-to-all(s16[16,32,128]{2,1,0:T(8,128)(2,1)S(1)} %strip.1), channel_id=1, replica_groups=mesh['grp'=2,'date'=16] {'date'}, dimensions={0} | all-to-all | bytes 262144 | tf_op jit(solution)/shard_map/all_to_all | solution.py:332
  30.6 0.8 %unpack.1 = (f32[6,8,512]{2,1,0:T(8,128)}, f32[6,8,512]{2,1,0:T(8,128)}) custom-call(s16[16,32,128]{2,1,0:T(8,128)(2,1)S(1)} %all_to_all.11.got_ref), custom_call_target="tpu_custom_call" | custom-call | tf_op jit(solution)/shard_map/unpack/pallas_call | solution.py:334

commit v5 on v4

--- a/solution.py
+++ b/solution.py
@@ -29,7 +29,37 @@
     return high, (x - high.astype(F32)).astype(BF16)
 
 
-def pack_kernel(mask_in, dev_in, slot_in, slc_in, out_ref, mask_ref, dev_ref, slot_ref, slc_ref, side_ref, sems):
+def make_table(width, table_ref):
+    blocks = LANES // width
+    me = lax.axis_index("date")
+
+    def main_place(shape, dim):
+        p = iota(shape, dim)
+        lane = p % LANES
+        k = (lane // width - me + 64) % blocks
+        line = jnp.where(k < 4, (p // LANES) * 4 + k, 1000 * (dim + 1))
+        return line, lane % width
+
+    def halo_place(shape, dim):
+        p = iota(shape, dim)
+        t = (p // 8 - me + 64) % 16
+        j = p % 8
+        return t % 8, jnp.where(j < HALO, j - HALO, width + j - HALO), t // 8
+
+    to_line, to_col = main_place((1, 2 * LANES), 1)
+
+    def near(line, col):
+        hit = (jnp.abs(line - to_line) <= 1) & (jnp.abs(col - to_col) <= HALO)
+        return hit.astype(F32)
+
+    table_ref[0:256, :] = near(*main_place((2 * LANES, 1), 0)).astype(BF16)
+    line, col, imag = halo_place((LANES, 1), 0)
+    halo = near(line, col)
+    table_ref[256:384, :] = halo.astype(BF16)
+    table_ref[384:512, :] = (halo * (2.0 * imag.astype(F32) - 1.0)).astype(BF16)
+
+
+def pack_kernel(mask_in, dev_in, slot_in, slc_in, out_ref, table_ref, mask_ref, dev_ref, slot_ref, slc_ref, side_ref, sems):
     step = slc_ref.shape[0] // 3
     copies = [
         pltpu.make_async_copy(source, target, sems.at[n])
@@ -47,6 +77,7 @@
     dates, _, rows, cols = slc_ref.shape
     width = cols // parts
     blocks = LANES // width
+    make_table(width, table_ref)
     place = iota((cols, 8 * parts), 1)
     j = place % 8
     column = (place // 8) * width + jnp.where(j < HALO, j - HALO, width + j - HALO)
@@ -113,13 +144,11 @@
 
 
 def strip_kernel(
-    dates, pair_count, width, chunk, got_ref, out_ref, first_ref, second_ref, diff_ref, diff_t_ref, weight_ref, term_ref
+    pair_count, chunk, got_ref, table_ref, out_ref, first_ref, second_ref, diff_ref, diff_t_ref, weight_ref, term_ref
 ):
     parts = got_ref.shape[0]
     slots = 8 * parts
-    blocks = LANES // width
     pairs = parts * pair_count
-    me = lax.axis_index("date")
 
     got = got_ref[...].astype(F32)
     group = [got[:, 8 * g : 8 * g + 8, :] for g in range(4)]
@@ -146,32 +175,9 @@
     diff_t = jnp.transpose(diff_ref[:, 0:slots].astype(F32)).astype(BF16)
     diff_t_ref[...] = jnp.concatenate([diff_t, diff_t], axis=1)
 
-    def main_place(shape, dim):
-        p = iota(shape, dim)
-        lane = p % LANES
-        k = (lane // width - me + 64) % blocks
-        line = jnp.where(k < 4, (p // LANES) * 4 + k, 1000 * (dim + 1))
-        return line, lane % width
-
-    def halo_place(shape, dim):
-        p = iota(shape, dim)
-        t = (p // 8 - me + 64) % 16
-        j = p % 8
-        return t % 8, jnp.where(j < HALO, j - HALO, width + j - HALO), t // 8
-
-    to_line, to_col = main_place((1, 2 * LANES), 1)
-
-    def near(line, col):
-        hit = (jnp.abs(line - to_line) <= 1) & (jnp.abs(col - to_col) <= HALO)
-        return hit.astype(F32)
-
-    band = near(*main_place((2 * LANES, 1), 0)).astype(BF16)
-    line, col, imag = halo_place((LANES, 1), 0)
-    band_halo = near(line, col)
-    band_cross = (band_halo * (2.0 * imag.astype(F32) - 1.0)).astype(BF16)
-    band_halo = band_halo.astype(BF16)
-    band_halo = jnp.concatenate([band, band, band_halo, band_halo], axis=0)
-    band_cross = jnp.concatenate([band, band, band_cross, band_cross], axis=0)
+    band, halo, cross = table_ref[0:256, :], table_ref[256:384, :], table_ref[384:512, :]
+    band_halo = jnp.concatenate([band, band, halo, halo], axis=0)
+    band_cross = jnp.concatenate([band, band, cross, cross], axis=0)
 
     def looks(field, edge, table):
         return dot(jnp.concatenate([*split(field), *split(edge)], axis=1), table)
@@ -291,11 +297,14 @@
     chunk = max(c for c in range(16, 513, 16) if pairs % c == 0)
     vmem = pl.BlockSpec(memory_space=pltpu.VMEM)
 
-    packed = pl.pallas_call(
+    packed, table = pl.pallas_call(
         pack_kernel,
-        out_shape=jax.ShapeDtypeStruct((parts, 32, LANES), BF16),
+        out_shape=(
+            jax.ShapeDtypeStruct((parts, 32, LANES), BF16),
+            jax.ShapeDtypeStruct((4 * LANES, 2 * LANES), BF16),
+        ),
         in_specs=[pl.BlockSpec(memory_space=pltpu.HBM)] * 4,
-        out_specs=vmem,
+        out_specs=(vmem, vmem),
         scratch_shapes=[
             pltpu.VMEM((dates, rows), jnp.int32),
             pltpu.VMEM((2, pair_count), jnp.int32),
@@ -314,9 +323,9 @@
     )
     got = lax.all_to_all(packed, "date", split_axis=0, concat_axis=0, tiled=True)
     fields = pl.pallas_call(
-        functools.partial(strip_kernel, dates, pair_count, width, chunk),
+        functools.partial(strip_kernel, pair_count, chunk),
         out_shape=jax.ShapeDtypeStruct((parts, 32, LANES), jnp.int16),
-        in_specs=[vmem],
+        in_specs=[vmem] * 2,
         out_specs=vmem,
         scratch_shapes=[
             pltpu.VMEM((pairs, 16 * parts), BF16),
@@ -328,7 +337,7 @@
         ],
         compiler_params=pltpu.CompilerParams(vmem_limit_bytes=24 * 1024 * 1024),
         name="strip",
-    )(got)
+    )(got, table)
     back = lax.all_to_all(fields, "date", split_axis=0, concat_axis=0, tiled=True)
     out = jax.ShapeDtypeStruct((dates, rows, cols), F32)
     return pl.pallas_call(

time: 31.8 us -> 31.5 us (level)
  no operation moved by 1% of the time
where the time goes in v5:
time: 31.5 us; the launch traced here: 31.2 us
  blocking collectives  25.6 us (81%)
  Pallas kernels  4.91 us (16%)
  between operations  0.65 us (2%)
    all_to_all x1, blocking collectives, shards(): lax.all_to_all(packed, 'date', split_axis=0, concat_axis=0, tiled=True)  15.1 us
    all_to_all x1, blocking collectives, shards(): lax.all_to_all(fields, 'date', split_axis=0, concat_axis=0, tiled=True)  10.5 us
    pallas_call x1, Pallas kernels, shards(): pl.pallas_call(functools.partial(strip_kernel, pair_count, chunk), out_sh...  2.76 us
    pallas_call x1, Pallas kernels, shards(): pl.pallas_call(pack_kernel, out_shape=(jax.ShapeDtypeStruct((parts, 32, L...  1.3 us
    pallas_call x1, Pallas kernels, shards(): pl.pallas_call(unpack_kernel, out_shape=(out, out), in_specs=[vmem], out_...  0.85 us

profile of v5, /device:TPU:0, one launch (start us, length us, event | category | flops | bytes accessed | tf_op | source)
XLA Modules:
  0.0 31.2 jit_solution(11653438764000242080)
XLA Ops:
  0.6 1.3 %pack.1 = (bf16[16,32,128]{2,1,0:T(8,128)(2,1)S(1)}, bf16[512,256]{1,0:T(8,128)(2,1)S(1)}) custom-call(s32[6,8]{1,0:T(8,128)} %mask_in.1, s32[2,25]{1,0:T(2,128)} %bitcast.2, s32[2,25]{1,0:T(2,128)} %bitcast.3, bf16[6,2,8,512]{3,2,1,0:T(8,128)(2,1)} %slc_in.1), custom_call_target="tpu_custom_call" | custom-call | tf_op jit(solution)/shard_map/pack/pallas_call | solution.py:300
  1.9 15.1 %all_to_all.10.got_ref = bf16[16,32,128]{2,1,0:T(8,128)(2,1)S(1)} all-to-all(bf16[16,32,128]{2,1,0:T(8,128)(2,1)S(1)} %get-tuple-element.4), channel_id=1, replica_groups=mesh['grp'=2,'date'=16] {'date'}, dimensions={0} | all-to-all | bytes 262144 | tf_op jit(solution)/shard_map/all_to_all | solution.py:324
  17.1 2.8 %strip.1 = s16[16,32,128]{2,1,0:T(8,128)(2,1)S(1)} custom-call(bf16[16,32,128]{2,1,0:T(8,128)(2,1)S(1)} %all_to_all.10.got_ref, bf16[512,256]{1,0:T(8,128)(2,1)S(1)} %get-tuple-element.5.table_ref), custom_call_target="tpu_custom_call" | custom-call | tf_op jit(solution)/shard_map/strip/pallas_call | solution.py:325
  19.8 10.5 %all_to_all.11.got_ref = s16[16,32,128]{2,1,0:T(8,128)(2,1)S(1)} all-to-all(s16[16,32,128]{2,1,0:T(8,128)(2,1)S(1)} %strip.1), channel_id=1, replica_groups=mesh['grp'=2,'date'=16] {'date'}, dimensions={0} | all-to-all | bytes 262144 | tf_op jit(solution)/shard_map/all_to_all | solution.py:341
  30.4 0.8 %unpack.1 = (f32[6,8,512]{2,1,0:T(8,128)}, f32[6,8,512]{2,1,0:T(8,128)}) custom-call(s16[16,32,128]{2,1,0:T(8,128)(2,1)S(1)} %all_to_all.11.got_ref), custom_call_target="tpu_custom_call" | custom-call | tf_op jit(solution)/shard_map/unpack/pallas_call | solution.py:343

commit v6 on v5

--- a/solution.py
+++ b/solution.py
@@ -172,8 +172,7 @@
         for ref, value in ((first_ref, first), (second_ref, second), (diff_ref, second - first)):
             value = value.astype(BF16)
             ref[at, :] = jnp.concatenate([value, value], axis=1)
-    diff_t = jnp.transpose(diff_ref[:, 0:slots].astype(F32)).astype(BF16)
-    diff_t_ref[...] = jnp.concatenate([diff_t, diff_t], axis=1)
+    diff_t_ref[...] = jnp.transpose(diff_ref[:, 0:slots].astype(F32)).astype(BF16)
 
     band, halo, cross = table_ref[0:256, :], table_ref[256:384, :], table_ref[384:512, :]
     band_halo = jnp.concatenate([band, band, halo, halo], axis=0)
@@ -186,31 +185,34 @@
     im = jnp.concatenate(columns[2:4], axis=1)
     power_high, power_low = split(looks(re * re + im * im, columns[4] * columns[4], band_halo))
     tiles = jnp.concatenate([x.astype(BF16) for x in columns], axis=1)
-    swap = pltpu.roll(columns[4], 64, 1).astype(BF16)
     zero = jnp.zeros_like(tiles)
-    first_tiles = jnp.concatenate(
+    both_tiles = jnp.concatenate(
         [
-            jnp.concatenate([power_high, tiles], axis=1),
-            jnp.concatenate([power_low, zero], axis=1),
+            jnp.concatenate([power_high, tiles[:, 0:512]], axis=1),
+            jnp.concatenate([power_low, zero[:, 0:512]], axis=1),
         ],
         axis=0,
     )
-    second_tiles = jnp.concatenate(
+    none = jnp.zeros((slots, LANES), BF16)
+    halo_tiles = jnp.concatenate(
         [
-            jnp.concatenate([power_high, tiles, swap], axis=1),
-            jnp.concatenate([power_low, zero, jnp.zeros_like(swap)], axis=1),
+            jnp.concatenate([tiles[:, 512:640], none], axis=1),
+            jnp.concatenate([none, tiles[:, 512:640]], axis=1),
         ],
         axis=0,
     )
 
     def body(step, carry):
         at = pl.ds(pl.multiple_of(step * chunk, 16), chunk)
-        u = dot(first_ref[at, :], first_tiles)
-        v = dot(second_ref[at, :], second_tiles)
-        u_power, u_re, u_im, u_halo = u[:, 0:256], u[:, 256:512], u[:, 512:768], u[:, 768:896]
-        v_power, v_re, v_im, v_halo = v[:, 0:256], v[:, 256:512], v[:, 512:768], v[:, 768:896]
+        u = dot(first_ref[at, :], both_tiles)
+        v = dot(second_ref[at, :], both_tiles)
+        u_power, u_re, u_im = u[:, 0:256], u[:, 256:512], u[:, 512:768]
+        v_power, v_re, v_im = v[:, 0:256], v[:, 256:512], v[:, 512:768]
+        either = jnp.concatenate([first_ref[at, 0:slots], second_ref[at, 0:slots]], axis=1)
+        halos = dot(either, halo_tiles)
+        u_halo, v_halo = halos[:, 0:128], halos[:, 128:256]
         real = looks(u_re * v_re + u_im * v_im, u_halo * v_halo, band_halo)
-        imag = looks(u_im * v_re - u_re * v_im, u_halo * v[:, 896:1024], band_cross)
+        imag = looks(u_im * v_re - u_re * v_im, u_halo * pltpu.roll(v_halo, 64, 1), band_cross)
         scale = lax.rsqrt(jnp.maximum(u_power * v_power, 1.0))
         real = real * scale
         imag = imag * scale
@@ -226,26 +228,35 @@
     else:
         lax.fori_loop(0, pairs // chunk, body, 0)
 
-    right_side = dot(diff_t_ref[...], term_ref[...])
+    right_side = dot(diff_t_ref[...], term_ref[0:pairs, :])
+    right_side = right_side + dot(diff_t_ref[...], term_ref[pairs : 2 * pairs, :])
+
+    def inner(a, b):
+        return jnp.sum(a * b, axis=0, keepdims=True)
+
+    half = -(-pairs // 32) * 16
+    halves = (slice(0, half), slice(half, pairs))
 
     def operator(field):
         high, low = split(field)
-        spread = dot(diff_ref[...], jnp.concatenate([high, low], axis=0))
-        high, low = split(weight_ref[...] * spread)
-        term_ref[0:pairs, :] = high
-        term_ref[pairs : 2 * pairs, :] = low
-        return DAMPING * field + dot(diff_t_ref[...], term_ref[...])
-
-    def inner(a, b):
-        return jnp.sum(a * b, axis=0, keepdims=True)
+        both = jnp.concatenate([high, low], axis=0)
+        image = DAMPING * field
+        curve = DAMPING * inner(field, field)
+        for at in halves:
+            spread = dot(diff_ref[at, :], both)
+            term = weight_ref[at, :] * spread
+            curve = curve + inner(term, spread)
+            high, low = split(term)
+            image = image + dot(diff_t_ref[:, at], high) + dot(diff_t_ref[:, at], low)
+        return image, curve
 
     solution = jnp.zeros_like(right_side)
     residual = right_side
     direction = right_side
     norm_now = inner(residual, residual)
     for step in range(ITERS):
-        image = operator(direction)
-        step_size = norm_now / (inner(direction, image) + EPSILON)
+        image, curve = operator(direction)
+        step_size = norm_now / (curve + EPSILON)
         solution = solution + step_size * direction
         residual = residual - step_size * image
         if step + 1 < ITERS:
@@ -274,6 +285,7 @@
     block = iota((8, LANES), 1) // width
     got = got_ref[...].astype(jnp.int32).astype(F32)
     for o, out_ref in enumerate(out_refs):
+        lines = [[] for _ in range(cols // LANES)]
         for h in range(2):
             at = (2 * o + h) * 8
             part = got[:, at : at + 8, :] * 2.0**-15 * jnp.exp2(got[:, at + 6 : at + 7, :])
@@ -285,7 +297,10 @@
                     shift = -width * k % LANES
                     if shift:
                         total = pltpu.roll(total, shift, 1)
-                    out_ref[:, 4 * h + k, tile * LANES : (tile + 1) * LANES] = total[0:dates]
+                    lines[tile].append(total)
+        for tile in range(cols // LANES):
+            whole = jnp.swapaxes(jnp.stack(lines[tile], axis=0), 0, 1)
+            out_ref[:, :, tile * LANES : (tile + 1) * LANES] = whole[0:dates]
 
 
 def shards(slc, line_mask, pair_dev, pair_slot):
@@ -331,7 +346,7 @@
             pltpu.VMEM((pairs, 16 * parts), BF16),
             pltpu.VMEM((pairs, 16 * parts), BF16),
             pltpu.VMEM((pairs, 16 * parts), BF16),
-            pltpu.VMEM((8 * parts, 2 * pairs), BF16),
+            pltpu.VMEM((8 * parts, pairs), BF16),
             pltpu.VMEM((pairs, 2 * LANES), F32),
             pltpu.VMEM((2 * pairs, 2 * LANES), BF16),
         ],

time: 31.5 us -> 31.2 us (level)
  no operation moved by 1% of the time
where the time goes in v6:
time: 31.2 us; the launch traced here: 30.9 us
  blocking collectives  25.6 us (82%)
  Pallas kernels  4.65 us (15%)
  between operations  0.64 us (2%)
    all_to_all x1, blocking collectives, shards(): lax.all_to_all(packed, 'date', split_axis=0, concat_axis=0, tiled=True)  15.1 us
    all_to_all x1, blocking collectives, shards(): lax.all_to_all(fields, 'date', split_axis=0, concat_axis=0, tiled=True)  10.5 us
    pallas_call x1, Pallas kernels, shards(): pl.pallas_call(functools.partial(strip_kernel, pair_count, chunk), out_sh...  2.55 us
    pallas_call x1, Pallas kernels, shards(): pl.pallas_call(pack_kernel, out_shape=(jax.ShapeDtypeStruct((parts, 32, L...  1.3 us
    pallas_call x1, Pallas kernels, shards(): pl.pallas_call(unpack_kernel, out_shape=(out, out), in_specs=[vmem], out_...  0.8 us

profile of v6, /device:TPU:0, one launch (start us, length us, event | category | flops | bytes accessed | tf_op | source)
XLA Modules:
  0.0 30.9 jit_solution(4071289893052362515)
XLA Ops:
  0.6 1.3 %pack.1 = (bf16[16,32,128]{2,1,0:T(8,128)(2,1)S(1)}, bf16[512,256]{1,0:T(8,128)(2,1)S(1)}) custom-call(s32[6,8]{1,0:T(8,128)} %mask_in.1, s32[2,25]{1,0:T(2,128)} %bitcast.2, s32[2,25]{1,0:T(2,128)} %bitcast.3, bf16[6,2,8,512]{3,2,1,0:T(8,128)(2,1)} %slc_in.1), custom_call_target="tpu_custom_call" | custom-call | tf_op jit(solution)/shard_map/pack/pallas_call | solution.py:315
  1.9 15.1 %all_to_all.10.got_ref = bf16[16,32,128]{2,1,0:T(8,128)(2,1)S(1)} all-to-all(bf16[16,32,128]{2,1,0:T(8,128)(2,1)S(1)} %get-tuple-element.4), channel_id=1, replica_groups=mesh['grp'=2,'date'=16] {'date'}, dimensions={0} | all-to-all | bytes 262144 | tf_op jit(solution)/shard_map/all_to_all | solution.py:339
  17.1 2.5 %strip.1 = s16[16,32,128]{2,1,0:T(8,128)(2,1)S(1)} custom-call(bf16[16,32,128]{2,1,0:T(8,128)(2,1)S(1)} %all_to_all.10.got_ref, bf16[512,256]{1,0:T(8,128)(2,1)S(1)} %get-tuple-element.5.table_ref), custom_call_target="tpu_custom_call" | custom-call | tf_op jit(solution)/shard_map/strip/pallas_call | solution.py:340
  19.6 10.5 %all_to_all.11.got_ref = s16[16,32,128]{2,1,0:T(8,128)(2,1)S(1)} all-to-all(s16[16,32,128]{2,1,0:T(8,128)(2,1)S(1)} %strip.1), channel_id=1, replica_groups=mesh['grp'=2,'date'=16] {'date'}, dimensions={0} | all-to-all | bytes 262144 | tf_op jit(solution)/shard_map/all_to_all | solution.py:356
  30.1 0.8 %unpack.1 = (f32[6,8,512]{2,1,0:T(8,128)}, f32[6,8,512]{2,1,0:T(8,128)}) custom-call(s16[16,32,128]{2,1,0:T(8,128)(2,1)S(1)} %all_to_all.11.got_ref), custom_call_target="tpu_custom_call" | custom-call | tf_op jit(solution)/shard_map/unpack/pallas_call | solution.py:358

commit v7 on v6

--- a/solution.py
+++ b/solution.py
@@ -263,18 +263,22 @@
             norm_next = inner(residual, residual)
             direction = residual + norm_next / (norm_now + EPSILON) * direction
             norm_now = norm_next
-    row = iota((parts, 8, LANES), 1)
-    groups = []
+    pieces = []
+    powers = []
     for field in (solution, residual):
         field = field.reshape(parts, 8, 2 * LANES)
+        largest = jnp.max(jnp.abs(field), axis=1, keepdims=True)
+        largest = jnp.maximum(largest[:, :, 0:LANES], largest[:, :, LANES : 2 * LANES])
+        power = jnp.floor(jnp.log2(jnp.maximum(largest, 2.0**-126))) + 1.0
+        powers.append(power)
+        scale = jnp.exp2(-power)
         for h in range(2):
             part = field[:, :, h * LANES : (h + 1) * LANES]
-            largest = jnp.max(jnp.abs(part), axis=1, keepdims=True)
-            power = jnp.floor(jnp.log2(jnp.maximum(largest, 2.0**-126))) + 1.0
-            coded = jnp.floor(part * jnp.exp2(-power) * 32768.0 + 0.5)
-            coded = jnp.where(row == 6, power, jnp.clip(coded, -32767.0, 32767.0))
-            groups.append(coded.astype(jnp.int32))
-    out_ref[...] = jnp.concatenate(groups, axis=1).astype(jnp.int16)
+            coded = jnp.floor(part * scale * 32768.0 + 0.5)
+            coded = jnp.clip(coded, -32767.0, 32767.0).astype(jnp.int32)
+            pieces += [coded[:, 2 * a : 2 * a + 2, :] for a in range(3)]
+    pieces.append(jnp.concatenate(powers, axis=1).astype(jnp.int32))
+    out_ref[...] = jnp.concatenate(pieces, axis=2).astype(jnp.int16)
 
 
 def unpack_kernel(got_ref, *out_refs):
@@ -284,11 +288,13 @@
     blocks = LANES // width
     block = iota((8, LANES), 1) // width
     got = got_ref[...].astype(jnp.int32).astype(F32)
+    none = jnp.zeros((parts, 2, LANES), F32)
     for o, out_ref in enumerate(out_refs):
         lines = [[] for _ in range(cols // LANES)]
+        scale = 2.0**-15 * jnp.exp2(got[:, o : o + 1, 12 * LANES : 13 * LANES])
         for h in range(2):
-            at = (2 * o + h) * 8
-            part = got[:, at : at + 8, :] * 2.0**-15 * jnp.exp2(got[:, at + 6 : at + 7, :])
+            at = [(6 * o + 3 * h + a) * LANES for a in range(3)]
+            part = jnp.concatenate([got[:, :, a : a + LANES] for a in at] + [none], axis=1) * scale
             for tile in range(cols // LANES):
                 for k in range(4):
                     total = jnp.zeros((8, LANES), F32)
@@ -339,7 +345,7 @@
     got = lax.all_to_all(packed, "date", split_axis=0, concat_axis=0, tiled=True)
     fields = pl.pallas_call(
         functools.partial(strip_kernel, pair_count, chunk),
-        out_shape=jax.ShapeDtypeStruct((parts, 32, LANES), jnp.int16),
+        out_shape=jax.ShapeDtypeStruct((parts, 2, 13 * LANES), jnp.int16),
         in_specs=[vmem] * 2,
         out_specs=vmem,
         scratch_shapes=[

time: 31.2 us -> 30.8 us (0.987)
  blocking collectives: 25.6 us -> 25.2 us
    all_to_all x1, blocking collectives: 10.5 us -> 10.1 us  [shards(): lax.all_to_all(fields, 'date', split_axis=0, concat_axis=0, tiled=True)]
where the time goes in v7:
time: 30.8 us; the launch traced here: 30.6 us
  blocking collectives  25.2 us (82%)
  Pallas kernels  4.69 us (15%)
  between operations  0.65 us (2%)
    all_to_all x1, blocking collectives, shards(): lax.all_to_all(packed, 'date', split_axis=0, concat_axis=0, tiled=True)  15.1 us
    all_to_all x1, blocking collectives, shards(): lax.all_to_all(fields, 'date', split_axis=0, concat_axis=0, tiled=True)  10.1 us
    pallas_call x1, Pallas kernels, shards(): pl.pallas_call(functools.partial(strip_kernel, pair_count, chunk), out_sh...  2.54 us
    pallas_call x1, Pallas kernels, shards(): pl.pallas_call(pack_kernel, out_shape=(jax.ShapeDtypeStruct((parts, 32, L...  1.3 us
    pallas_call x1, Pallas kernels, shards(): pl.pallas_call(unpack_kernel, out_shape=(out, out), in_specs=[vmem], out_...  0.85 us

profile of v7, /device:TPU:0, one launch (start us, length us, event | category | flops | bytes accessed | tf_op | source)
XLA Modules:
  0.0 30.6 jit_solution(7004891544363597967)
XLA Ops:
  0.6 1.3 %pack.1 = (bf16[16,32,128]{2,1,0:T(8,128)(2,1)S(1)}, bf16[512,256]{1,0:T(8,128)(2,1)S(1)}) custom-call(s32[6,8]{1,0:T(8,128)} %mask_in.1, s32[2,25]{1,0:T(2,128)} %bitcast.2, s32[2,25]{1,0:T(2,128)} %bitcast.3, bf16[6,2,8,512]{3,2,1,0:T(8,128)(2,1)} %slc_in.1), custom_call_target="tpu_custom_call" | custom-call | tf_op jit(solution)/shard_map/pack/pallas_call | solution.py:321
  1.9 15.1 %all_to_all.10.got_ref = bf16[16,32,128]{2,1,0:T(8,128)(2,1)S(1)} all-to-all(bf16[16,32,128]{2,1,0:T(8,128)(2,1)S(1)} %get-tuple-element.4), channel_id=1, replica_groups=mesh['grp'=2,'date'=16] {'date'}, dimensions={0} | all-to-all | bytes 262144 | tf_op jit(solution)/shard_map/all_to_all | solution.py:345
  17.1 2.5 %strip.1 = s16[16,2,1664]{2,1,0:T(2,128)(2,1)S(1)} custom-call(bf16[16,32,128]{2,1,0:T(8,128)(2,1)S(1)} %all_to_all.10.got_ref, bf16[512,256]{1,0:T(8,128)(2,1)S(1)} %get-tuple-element.5.table_ref), custom_call_target="tpu_custom_call" | custom-call | tf_op jit(solution)/shard_map/strip/pallas_call | solution.py:346
  19.6 10.1 %all_to_all.11.got_ref = s16[16,2,1664]{2,1,0:T(2,128)(2,1)S(1)} all-to-all(s16[16,2,1664]{2,1,0:T(2,128)(2,1)S(1)} %strip.1), channel_id=1, replica_groups=mesh['grp'=2,'date'=16] {'date'}, dimensions={0} | all-to-all | bytes 212992 | tf_op jit(solution)/shard_map/all_to_all | solution.py:362
  29.7 0.8 %unpack.1 = (f32[6,8,512]{2,1,0:T(8,128)}, f32[6,8,512]{2,1,0:T(8,128)}) custom-call(s16[16,2,1664]{2,1,0:T(2,128)(2,1)S(1)} %all_to_all.11.got_ref), custom_call_target="tpu_custom_call" | custom-call | tf_op jit(solution)/shard_map/unpack/pallas_call | solution.py:364

commit v8 on v7

--- a/solution.py
+++ b/solution.py
@@ -84,21 +84,44 @@
     side_ref[...] = (iota((cols, 8 * parts), 0) == column).astype(F32).astype(BF16)
     for copy in copies[:3]:
         copy.wait()
-    mask = jnp.concatenate(
-        [mask_ref[...].astype(F32), jnp.zeros((8 - dates, rows), F32)], axis=0
-    )
-    lane = iota((8, dates * 2 * rows), 1)
-    row = iota((8, dates * 2 * rows), 0)
-    picks = []
-    for i in range(rows):
-        for c in range(2):
-            picks.append(jnp.where(lane == (row * 2 + c) * rows + i, mask[:, i : i + 1], 0.0))
-    pick = jnp.concatenate(picks, axis=0).astype(BF16)
+    mask = mask_ref[...].astype(F32)
+    diagonal = iota((rows, rows), 0) == iota((rows, rows), 1)
+    valid = [
+        jnp.sum(jnp.where(diagonal, mask[a : a + 1, :], 0.0), axis=1, keepdims=True)
+        for a in range(dates)
+    ]
     for copy in copies[3:]:
         copy.wait()
-    tiles = slc_ref[...].astype(F32).reshape(dates * 2 * rows, cols).astype(BF16)
-    lines = dot(pick, tiles)
-    edges = dot(lines.astype(BF16), side_ref[...])
+    tiles = [
+        [slc_ref[a, c].astype(F32) * valid[a] for c in range(2)] for a in range(dates)
+    ]
+    stacked = jnp.concatenate([x for pair in tiles for x in pair], axis=0)
+    edges = dot(stacked.astype(BF16), side_ref[...])
+    empty = jnp.zeros((rows, LANES), F32)
+
+    def by_line(parts_of_dates):
+        whole = jnp.stack(parts_of_dates + [empty] * (8 - dates), axis=0)
+        return jnp.swapaxes(whole, 0, 1)
+
+    lines = [
+        [
+            by_line([tiles[a][c][:, t * LANES : (t + 1) * LANES] for a in range(dates)])
+            for t in range(cols // LANES)
+        ]
+        for c in range(2)
+    ]
+    edges = [
+        [
+            by_line(
+                [
+                    edges[(2 * a + c) * rows : (2 * a + c + 1) * rows, t * LANES : (t + 1) * LANES]
+                    for a in range(dates)
+                ]
+            )
+            for t in range(8 * parts // LANES)
+        ]
+        for c in range(2)
+    ]
 
     lane = iota((8, LANES), 1)
     row = iota((8, LANES), 0)
@@ -112,8 +135,7 @@
     index_rows = jnp.concatenate([jnp.zeros((6, LANES), F32), index_rows], axis=0)
 
     def rolled(array, i, c, tile, shift):
-        at = (i * 2 + c) * 8
-        part = array[at : at + 8, tile * LANES : (tile + 1) * LANES]
+        part = array[c][tile][i]
         return part if shift % LANES == 0 else pltpu.roll(part, shift % LANES, 1)
 
     for tile in range(cols // LANES):

time: 30.8 us -> 30.8 us (level)
  no operation moved by 1% of the time
where the time goes in v8:
time: 30.8 us; the launch traced here: 30.5 us
  blocking collectives  25.2 us (82%)
  Pallas kernels  4.6 us (15%)
  between operations  0.65 us (2%)
    all_to_all x1, blocking collectives, shards(): lax.all_to_all(packed, 'date', split_axis=0, concat_axis=0, tiled=True)  15.1 us
    all_to_all x1, blocking collectives, shards(): lax.all_to_all(fields, 'date', split_axis=0, concat_axis=0, tiled=True)  10.1 us
    pallas_call x1, Pallas kernels, shards(): pl.pallas_call(functools.partial(strip_kernel, pair_count, chunk), out_sh...  2.54 us
    pallas_call x1, Pallas kernels, shards(): pl.pallas_call(pack_kernel, out_shape=(jax.ShapeDtypeStruct((parts, 32, L...  1.21 us
    pallas_call x1, Pallas kernels, shards(): pl.pallas_call(unpack_kernel, out_shape=(out, out), in_specs=[vmem], out_...  0.85 us

profile of v8, /device:TPU:0, one launch (start us, length us, event | category | flops | bytes accessed | tf_op | source)
XLA Modules:
  0.0 30.5 jit_solution(10066102889329173373)
XLA Ops:
  0.6 1.2 %pack.1 = (bf16[16,32,128]{2,1,0:T(8,128)(2,1)S(1)}, bf16[512,256]{1,0:T(8,128)(2,1)S(1)}) custom-call(s32[6,8]{1,0:T(8,128)} %mask_in.1, s32[2,25]{1,0:T(2,128)} %bitcast.2, s32[2,25]{1,0:T(2,128)} %bitcast.3, bf16[6,2,8,512]{3,2,1,0:T(8,128)(2,1)} %slc_in.1), custom_call_target="tpu_custom_call" | custom-call | tf_op jit(solution)/shard_map/pack/pallas_call | solution.py:343
  1.8 15.1 %all_to_all.10.got_ref = bf16[16,32,128]{2,1,0:T(8,128)(2,1)S(1)} all-to-all(bf16[16,32,128]{2,1,0:T(8,128)(2,1)S(1)} %get-tuple-element.4), channel_id=1, replica_groups=mesh['grp'=2,'date'=16] {'date'}, dimensions={0} | all-to-all | bytes 262144 | tf_op jit(solution)/shard_map/all_to_all | solution.py:367
  17.0 2.5 %strip.1 = s16[16,2,1664]{2,1,0:T(2,128)(2,1)S(1)} custom-call(bf16[16,32,128]{2,1,0:T(8,128)(2,1)S(1)} %all_to_all.10.got_ref, bf16[512,256]{1,0:T(8,128)(2,1)S(1)} %get-tuple-element.5.table_ref), custom_call_target="tpu_custom_call" | custom-call | tf_op jit(solution)/shard_map/strip/pallas_call | solution.py:368
  19.5 10.1 %all_to_all.11.got_ref = s16[16,2,1664]{2,1,0:T(2,128)(2,1)S(1)} all-to-all(s16[16,2,1664]{2,1,0:T(2,128)(2,1)S(1)} %strip.1), channel_id=1, replica_groups=mesh['grp'=2,'date'=16] {'date'}, dimensions={0} | all-to-all | bytes 212992 | tf_op jit(solution)/shard_map/all_to_all | solution.py:384
  29.6 0.8 %unpack.1 = (f32[6,8,512]{2,1,0:T(8,128)}, f32[6,8,512]{2,1,0:T(8,128)}) custom-call(s16[16,2,1664]{2,1,0:T(2,128)(2,1)S(1)} %all_to_all.11.got_ref), custom_call_target="tpu_custom_call" | custom-call | tf_op jit(solution)/shard_map/unpack/pallas_call | solution.py:386

commit v9 on v8

--- a/solution.py
+++ b/solution.py
@@ -259,11 +259,11 @@
     half = -(-pairs // 32) * 16
     halves = (slice(0, half), slice(half, pairs))
 
-    def operator(field):
+    def operator(field, square):
         high, low = split(field)
         both = jnp.concatenate([high, low], axis=0)
         image = DAMPING * field
-        curve = DAMPING * inner(field, field)
+        curve = DAMPING * square
         for at in halves:
             spread = dot(diff_ref[at, :], both)
             term = weight_ref[at, :] * spread
@@ -276,14 +276,16 @@
     residual = right_side
     direction = right_side
     norm_now = inner(residual, residual)
+    square = norm_now
     for step in range(ITERS):
-        image, curve = operator(direction)
+        image, curve = operator(direction, square)
         step_size = norm_now / (curve + EPSILON)
         solution = solution + step_size * direction
         residual = residual - step_size * image
         if step + 1 < ITERS:
             norm_next = inner(residual, residual)
             direction = residual + norm_next / (norm_now + EPSILON) * direction
+            square = inner(direction, direction)
             norm_now = norm_next
     pieces = []
     powers = []
@@ -313,10 +315,11 @@
     none = jnp.zeros((parts, 2, LANES), F32)
     for o, out_ref in enumerate(out_refs):
         lines = [[] for _ in range(cols // LANES)]
-        scale = 2.0**-15 * jnp.exp2(got[:, o : o + 1, 12 * LANES : 13 * LANES])
+        scale = jnp.exp2(got[:, o : o + 1, 12 * LANES : 13 * LANES])
         for h in range(2):
             at = [(6 * o + 3 * h + a) * LANES for a in range(3)]
-            part = jnp.concatenate([got[:, :, a : a + LANES] for a in at] + [none], axis=1) * scale
+            part = jnp.concatenate([got[:, :, a : a + LANES] for a in at] + [none], axis=1)
+            part = part * 2.0**-15 * scale
             for tile in range(cols // LANES):
                 for k in range(4):
                     total = jnp.zeros((8, LANES), F32)

time: 30.8 us -> 30.8 us (level)
  no operation moved by 1% of the time
where the time goes in v9:
time: 30.8 us; the launch traced here: 30.5 us
  blocking collectives  25.2 us (82%)
  Pallas kernels  4.61 us (15%)
  between operations  0.65 us (2%)
    all_to_all x1, blocking collectives, shards(): lax.all_to_all(packed, 'date', split_axis=0, concat_axis=0, tiled=True)  15.1 us
    all_to_all x1, blocking collectives, shards(): lax.all_to_all(fields, 'date', split_axis=0, concat_axis=0, tiled=True)  10.1 us
    pallas_call x1, Pallas kernels, shards(): pl.pallas_call(functools.partial(strip_kernel, pair_count, chunk), out_sh...  2.54 us
    pallas_call x1, Pallas kernels, shards(): pl.pallas_call(pack_kernel, out_shape=(jax.ShapeDtypeStruct((parts, 32, L...  1.21 us
    pallas_call x1, Pallas kernels, shards(): pl.pallas_call(unpack_kernel, out_shape=(out, out), in_specs=[vmem], out_...  0.86 us

profile of v9, /device:TPU:0, one launch (start us, length us, event | category | flops | bytes accessed | tf_op | source)
XLA Modules:
  0.0 30.5 jit_solution(11176084075063574676)
XLA Ops:
  0.6 1.2 %pack.1 = (bf16[16,32,128]{2,1,0:T(8,128)(2,1)S(1)}, bf16[512,256]{1,0:T(8,128)(2,1)S(1)}) custom-call(s32[6,8]{1,0:T(8,128)} %mask_in.1, s32[2,25]{1,0:T(2,128)} %bitcast.2, s32[2,25]{1,0:T(2,128)} %bitcast.3, bf16[6,2,8,512]{3,2,1,0:T(8,128)(2,1)} %slc_in.1), custom_call_target="tpu_custom_call" | custom-call | tf_op jit(solution)/shard_map/pack/pallas_call | solution.py:346
  1.8 15.1 %all_to_all.10.got_ref = bf16[16,32,128]{2,1,0:T(8,128)(2,1)S(1)} all-to-all(bf16[16,32,128]{2,1,0:T(8,128)(2,1)S(1)} %get-tuple-element.4), channel_id=1, replica_groups=mesh['grp'=2,'date'=16] {'date'}, dimensions={0} | all-to-all | bytes 262144 | tf_op jit(solution)/shard_map/all_to_all | solution.py:370
  17.0 2.5 %strip.1 = s16[16,2,1664]{2,1,0:T(2,128)(2,1)S(1)} custom-call(bf16[16,32,128]{2,1,0:T(8,128)(2,1)S(1)} %all_to_all.10.got_ref, bf16[512,256]{1,0:T(8,128)(2,1)S(1)} %get-tuple-element.5.table_ref), custom_call_target="tpu_custom_call" | custom-call | tf_op jit(solution)/shard_map/strip/pallas_call | solution.py:371
  19.5 10.1 %all_to_all.11.got_ref = s16[16,2,1664]{2,1,0:T(2,128)(2,1)S(1)} all-to-all(s16[16,2,1664]{2,1,0:T(2,128)(2,1)S(1)} %strip.1), channel_id=1, replica_groups=mesh['grp'=2,'date'=16] {'date'}, dimensions={0} | all-to-all | bytes 212992 | tf_op jit(solution)/shard_map/all_to_all | solution.py:387
  29.6 0.9 %unpack.1 = (f32[6,8,512]{2,1,0:T(8,128)}, f32[6,8,512]{2,1,0:T(8,128)}) custom-call(s16[16,2,1664]{2,1,0:T(2,128)(2,1)S(1)} %all_to_all.11.got_ref), custom_call_target="tpu_custom_call" | custom-call | tf_op jit(solution)/shard_map/unpack/pallas_call | solution.py:389

commit v10 on v9

--- a/solution.py
+++ b/solution.py
@@ -71,8 +71,8 @@
             ]
         )
     ]
-    for copy in copies:
-        copy.start()
+    for n, copy in enumerate(copies):
+        copy.start(priority=n % 2)
     parts = out_ref.shape[0]
     dates, _, rows, cols = slc_ref.shape
     width = cols // parts
@@ -95,8 +95,8 @@
     tiles = [
         [slc_ref[a, c].astype(F32) * valid[a] for c in range(2)] for a in range(dates)
     ]
-    stacked = jnp.concatenate([x for pair in tiles for x in pair], axis=0)
-    edges = dot(stacked.astype(BF16), side_ref[...])
+    raw = slc_ref[...].astype(F32).reshape(dates * 2 * rows, cols).astype(BF16)
+    edges = dot(raw, side_ref[...])
     empty = jnp.zeros((rows, LANES), F32)
 
     def by_line(parts_of_dates):
@@ -115,6 +115,7 @@
             by_line(
                 [
                     edges[(2 * a + c) * rows : (2 * a + c + 1) * rows, t * LANES : (t + 1) * LANES]
+                    * valid[a]
                     for a in range(dates)
                 ]
             )
@@ -224,6 +225,12 @@
         axis=0,
     )
 
+    half = -(-pairs // 32) * 16
+    halves = (slice(0, half), slice(half, pairs))
+
+    def scatter(high, low):
+        return sum(dot(diff_t_ref[:, at], x[at]) for at in halves for x in (high, low))
+
     def body(step, carry):
         at = pl.ds(pl.multiple_of(step * chunk, 16), chunk)
         u = dot(first_ref[at, :], both_tiles)
@@ -241,23 +248,21 @@
         weight = real * real + imag * imag
         weight_ref[at, :] = weight
         high, low = split(weight * imag)
+        if chunk == pairs:
+            return scatter(high, low)
         term_ref[at, :] = high
         term_ref[pl.ds(pl.multiple_of(pairs + step * chunk, 16), chunk), :] = low
         return carry
 
     if chunk == pairs:
-        body(0, 0)
+        right_side = body(0, 0)
     else:
         lax.fori_loop(0, pairs // chunk, body, 0)
-
-    right_side = dot(diff_t_ref[...], term_ref[0:pairs, :])
-    right_side = right_side + dot(diff_t_ref[...], term_ref[pairs : 2 * pairs, :])
+        right_side = scatter(term_ref[0:pairs, :], term_ref[pairs : 2 * pairs, :])
+
 
     def inner(a, b):
         return jnp.sum(a * b, axis=0, keepdims=True)
-
-    half = -(-pairs // 32) * 16
-    halves = (slice(0, half), slice(half, pairs))
 
     def operator(field, square):
         high, low = split(field)

time: 30.8 us -> 30.8 us (level)
  no operation moved by 1% of the time
where the time goes in v10:
time: 30.8 us; the launch traced here: 30.5 us
  blocking collectives  25.2 us (82%)
  Pallas kernels  4.6 us (15%)
  between operations  0.64 us (2%)
    all_to_all x1, blocking collectives, shards(): lax.all_to_all(packed, 'date', split_axis=0, concat_axis=0, tiled=True)  15.1 us
    all_to_all x1, blocking collectives, shards(): lax.all_to_all(fields, 'date', split_axis=0, concat_axis=0, tiled=True)  10.1 us
    pallas_call x1, Pallas kernels, shards(): pl.pallas_call(functools.partial(strip_kernel, pair_count, chunk), out_sh...  2.53 us
    pallas_call x1, Pallas kernels, shards(): pl.pallas_call(pack_kernel, out_shape=(jax.ShapeDtypeStruct((parts, 32, L...  1.21 us
    pallas_call x1, Pallas kernels, shards(): pl.pallas_call(unpack_kernel, out_shape=(out, out), in_specs=[vmem], out_...  0.86 us

profile of v10, /device:TPU:0, one launch (start us, length us, event | category | flops | bytes accessed | tf_op | source)
XLA Modules:
  0.0 30.5 jit_solution(4568300569674309932)
XLA Ops:
  0.6 1.2 %pack.1 = (bf16[16,32,128]{2,1,0:T(8,128)(2,1)S(1)}, bf16[512,256]{1,0:T(8,128)(2,1)S(1)}) custom-call(s32[6,8]{1,0:T(8,128)} %mask_in.1, s32[2,25]{1,0:T(2,128)} %bitcast.2, s32[2,25]{1,0:T(2,128)} %bitcast.3, bf16[6,2,8,512]{3,2,1,0:T(8,128)(2,1)} %slc_in.1), custom_call_target="tpu_custom_call" | custom-call | tf_op jit(solution)/shard_map/pack/pallas_call | solution.py:351
  1.8 15.1 %all_to_all.10.got_ref = bf16[16,32,128]{2,1,0:T(8,128)(2,1)S(1)} all-to-all(bf16[16,32,128]{2,1,0:T(8,128)(2,1)S(1)} %get-tuple-element.4), channel_id=1, replica_groups=mesh['grp'=2,'date'=16] {'date'}, dimensions={0} | all-to-all | bytes 262144 | tf_op jit(solution)/shard_map/all_to_all | solution.py:375
  17.0 2.5 %strip.1 = s16[16,2,1664]{2,1,0:T(2,128)(2,1)S(1)} custom-call(bf16[16,32,128]{2,1,0:T(8,128)(2,1)S(1)} %all_to_all.10.got_ref, bf16[512,256]{1,0:T(8,128)(2,1)S(1)} %get-tuple-element.5.table_ref), custom_call_target="tpu_custom_call" | custom-call | tf_op jit(solution)/shard_map/strip/pallas_call | solution.py:376
  19.5 10.1 %all_to_all.11.got_ref = s16[16,2,1664]{2,1,0:T(2,128)(2,1)S(1)} all-to-all(s16[16,2,1664]{2,1,0:T(2,128)(2,1)S(1)} %strip.1), channel_id=1, replica_groups=mesh['grp'=2,'date'=16] {'date'}, dimensions={0} | all-to-all | bytes 212992 | tf_op jit(solution)/shard_map/all_to_all | solution.py:392
  29.6 0.9 %unpack.1 = (f32[6,8,512]{2,1,0:T(8,128)}, f32[6,8,512]{2,1,0:T(8,128)}) custom-call(s16[16,2,1664]{2,1,0:T(2,128)(2,1)S(1)} %all_to_all.11.got_ref), custom_call_target="tpu_custom_call" | custom-call | tf_op jit(solution)/shard_map/unpack/pallas_call | solution.py:394
